TPU v7x, 256 devices: a whole 4x4x8 slice. The times are simulated.
256 devices in a mesh: lvl: 4 (over y), cell: 64 (over x, z, core).
Axes of the slice: x: 4, y: 4, z: 8, core: 2. Of those that a mesh axis runs over, the one named last changes fastest.
Arguments:
- rhs: float32 [16, 1024, 1024], P('lvl', 'cell'), may hold values from -6 to 6
- adjoint_owned: float32 [16, 1024, 1024], P('lvl', 'cell'), may hold values from -6 to 6
- owner_of: int32 [16, 1024], P('lvl', 'cell'), may hold values from 0 to 16383, as said below
- columns: int32 [16, 1024, 3], P('lvl', 'cell'), may hold values from 0 to 1023, as said below
- lower: float32 [16, 1024, 3, 4096], P('lvl', 'cell'), may hold values from -0.4375 to 0.4375
- dinv: float32 [16, 1024, 4096], P('lvl', 'cell'), may hold values from -0.3 to 1, as said below
Outputs:
- solved: float32 [16, 1024, 1024], P('lvl', 'cell')
- adjoint: float32 [16, 1024, 1024], P('lvl', 'cell')
Inputs may be any that keep to these rules, and one draw needn't show every extreme that they name: `columns`: entry k of block row q of level l names a row of level l - 1 whose position differs from q by at most 8 cyclically over 1024 rows; the 3 entries of a row differ. `owner_of`: A permutation that keeps each section of 4 consecutive levels within itself. Numbering a device's owner positions m = (level mod 4) * 16 + (row mod 16), the block row q of level order sits at an owner position whose m, modulo the number of devices along cell, equals q // 16. `dinv`: diagonal entries of each block between 0.6 and 1.
All inputs are finite; a program needn't handle non-finite values.
Results may differ from a plain program's by a relative error of at most 0.00011.
Values sent between devices are 32-bit elements; how exact they have to be, the bound alone decides.
No kernel may reach another device: no remote copies, remote signals or barrier semaphores. Data moves between devices by JAX's collectives and lax.ppermute only.
A program may use at most 192 MiB of HBM per device.

v0:
```python
from functools import partial

import jax
import jax.numpy as jnp
from jax import lax
from jax.experimental import pallas as pl
from jax.experimental.pallas import tpu as pltpu
from jax.sharding import PartitionSpec as P

B = 64
NV = 16
K = 3
W = 8
LV = 4
RL = 16
ROWS = LV * RL
EXT = RL + 2 * W
VMEM = pltpu.VMEM
SMEM = pltpu.SMEM
F32 = jnp.float32
BF16 = jnp.bfloat16
MIB = 1 << 20


def in_vmem(x):
    return pltpu.with_memory_space_constraint(x, VMEM)


def in_hbm(x):
    return pltpu.with_memory_space_constraint(x, pltpu.HBM)


def in_smem(x):
    return pltpu.with_memory_space_constraint(x, SMEM)


def split(x):
    hi = x.astype(BF16)
    lo = (x - hi.astype(F32)).astype(BF16)
    return hi, lo


def nn(a, b):
    return jnp.dot(a, b, preferred_element_type=F32)


def nt(a, b):
    return lax.dot_general(a, b, (((1,), (1,)), ((), ())), preferred_element_type=F32)


def low_half(shape):
    return lax.broadcasted_iota(jnp.int32, shape, len(shape) - 1) % 128 < B


def other_half(x):
    return pltpu.roll(x, B, axis=x.ndim - 1)


def spread_matrix():
    row = lax.broadcasted_iota(jnp.int32, (B * NV, 128), 0) // NV
    col = lax.broadcasted_iota(jnp.int32, (B * NV, 128), 1) % B
    return jnp.where(row == col, 1.0, 0.0).astype(BF16)


def own_lane(rows):
    lane = lax.broadcasted_iota(jnp.int32, (rows, 128), 1) % NV
    vec = lax.broadcasted_iota(jnp.int32, (rows, 128), 0) % NV
    return lane == vec


def state_of_rows(load, wide_hi, wide_lo):
    mask = own_lane(NV)

    def one(row, carry):
        block = load(row)
        for chunk in range(B * NV // 128):
            value = jnp.broadcast_to(block[chunk:chunk + 1], (NV, 128))
            hi, lo = split(jnp.where(mask, value, 0.0))
            place = (pl.ds(pl.multiple_of(row * NV, NV), NV), pl.ds(chunk * 128, 128))
            wide_hi[place] = hi
            wide_lo[place] = lo
        return carry

    lax.fori_loop(0, RL, one, 0, unroll=2)
    row = lax.broadcasted_iota(jnp.int32, (256, 128), 0) // NV
    col = lax.broadcasted_iota(jnp.int32, (256, 128), 1) % B

    def add(part, total):
        spread = jnp.where(row + part * (256 // NV) == col, 1.0, 0.0).astype(BF16)
        lanes = pl.ds(pl.multiple_of(part * 256, 256), 256)
        return total + nn(wide_hi[:, lanes], spread) + nn(wide_lo[:, lanes], spread)

    out = lax.fori_loop(0, B * NV // 256, add, jnp.zeros((RL * NV, 128), F32))
    return out.reshape(RL, NV, 128)


def storage_level(part):
    section = lax.axis_index("lvl")
    return jnp.where(section < LV // 2, part, LV - 1 - part)


def relay_kernel(owned_hbm, columns_hbm, owner_hbm, sent_hbm, s_ref,
                 table, turn, owned_ref, columns_ref, owner_ref, sent_rows, sems):
    arrivals = [
        pltpu.make_async_copy(owned_hbm, owned_ref, sems.at[0]),
        pltpu.make_async_copy(columns_hbm, columns_ref, sems.at[1]),
        pltpu.make_async_copy(owner_hbm, owner_ref, sems.at[2]),
    ]
    for copy in arrivals:
        copy.start()
    for copy in arrivals:
        copy.wait()
    for group in range(ROWS // 8):
        base = group % 2 * 8
        for chunk in range(B * NV // 128):
            turn[group, pl.ds(chunk * 8, 8), :] = owned_ref[group // 2, base:base + 8, chunk * 128:(chunk + 1) * 128]
        for row in range(8):
            sent_rows[group * 8 + row] = turn[group, pl.ds(row, B * NV // 128, stride=8), :]
    sent_copy = pltpu.make_async_copy(sent_rows, sent_hbm, sems.at[3])
    sent_copy.start()
    cells = lax.axis_size("cell")
    span = RL * cells
    local = lax.broadcasted_iota(jnp.int32, columns_ref.shape, 2)
    offset = columns_ref[...] - local - lax.axis_index("cell") * RL
    offset = jnp.where(offset > span // 2, offset - span, offset)
    offset = jnp.where(offset < -(span // 2), offset + span, offset)
    place = jnp.clip(offset + local + W, 0, EXT - 1)
    for k in range(K):
        table[pl.ds(k * LV, LV), pl.ds(0, RL)] = place[k]
    owner = owner_ref[...]
    owner_row = owner % span
    owner_local = owner // span % LV * RL + owner_row % RL
    table[pl.ds(K * LV, LV), pl.ds(0, RL)] = owner_local // cells * cells + owner_row // RL
    table_copy = pltpu.make_async_copy(table, s_ref, sems.at[4])
    table_copy.start()
    table_copy.wait()
    sent_copy.wait()


def blocks_kernel(part, lower_hbm, dinv_hbm, rhs_hbm, w_ref, r_ref,
                  low, din, tiles, both, sems, wide_hi, wide_lo, rhs_ref, lines):
    level = storage_level(part)
    rhs_copy = pltpu.make_async_copy(rhs_hbm.at[level], rhs_ref, sems.at[2])
    copies = (
        pltpu.make_async_copy(lower_hbm.at[level], low, sems.at[0]),
        pltpu.make_async_copy(dinv_hbm.at[level], din, sems.at[1]),
    )
    for copy in (rhs_copy, *copies):
        copy.start()
    rhs_copy.wait()

    for half in range(2):
        for chunk in range(B * NV // 128):
            lines[half, pl.ds(chunk * 8, 8), :] = rhs_ref[half * 8:half * 8 + 8, chunk * 128:(chunk + 1) * 128]

    def load_rhs(row):
        return lines[row // 8, pl.ds(row % 8, B * NV // 128, stride=8), :]

    r_ref[...] = state_of_rows(load_rhs, wide_hi, wide_lo)
    left = low_half((B // 2, 128))
    left_wide = low_half((B, 128))
    for copy in copies:
        copy.wait()
    def turn_half(half, carry):
        start = pl.multiple_of(half * 8, 8)
        for k in range(K + 1):
            for chunk in range(B * B // 128):
                lanes = pl.ds(chunk * 128, 128)
                value = low[k, pl.ds(start, 8), lanes] if k < K else din[pl.ds(start, 8), lanes]
                tiles[half, k, pl.ds(chunk * 8, 8), :] = value
        return carry

    lax.fori_loop(0, 2, turn_half, 0)

    def row_blocks(half, row, slot):
        piece = [tiles[half, k, pl.ds(row, B // 2, stride=8), :] for k in range(K + 1)]
        turned = [other_half(p) for p in piece]
        both[slot, 0, pl.ds(0, B // 2, stride=2), :] = jnp.where(left, piece[0], turned[1])
        both[slot, 0, pl.ds(1, B // 2, stride=2), :] = jnp.where(left, turned[0], piece[1])
        both[slot, 1, pl.ds(0, B // 2, stride=2), :] = jnp.where(left, piece[2], turned[3])
        both[slot, 1, pl.ds(1, B // 2, stride=2), :] = jnp.where(left, turned[2], piece[3])
        first_tile, second = both[slot, 0], both[slot, 1]
        diag = other_half(second)[:, :B]
        diag_hi, diag_lo = split(diag)
        right_hi, right_lo = split(jnp.concatenate([first_tile, second], axis=1))
        top = nn(jnp.concatenate([diag_hi, diag_lo], axis=0), right_hi)
        product = top[:B] + top[B:] + nn(diag_hi, right_lo)
        tail = jnp.where(left_wide, product[:, 128:], second)
        hi, lo = split(jnp.concatenate([product[:, :128], tail], axis=1))
        w_ref[half * 8 + row] = jnp.concatenate([hi, lo], axis=0)

    def two_rows(pair, carry):
        for row in range(2):
            row_blocks(pair // 4, pair % 4 * 2 + row, row)
        return carry

    lax.fori_loop(0, RL // 2, two_rows, 0)


def adjoint_kernel(parts, s_ref, relayed_ref, *refs):
    *outs, wide_hi, wide_lo = refs
    for part, a_ref in zip(parts, outs):
        level = storage_level(part)

        def load(row):
            return relayed_ref[s_ref[K * LV + level, row]]

        a_ref[...] = state_of_rows(load, wide_hi, wide_lo)


def pack(x):
    half = x.shape[0] // 2
    return jnp.where(low_half((half, NV, 128)), x[:half], x[half:])


def unpack(x):
    turned = other_half(x)
    left = low_half(x.shape)
    return jnp.concatenate([jnp.where(left, x, turned), jnp.where(left, turned, x)], axis=0)


def is_even():
    return lax.axis_index("cell") % 2 == 0


def by_side(near, far, do):
    even = is_even()
    pl.when(even)(lambda: do(far, near))
    pl.when(jnp.logical_not(even))(lambda: do(near, far))


def in_eights(count, do):
    def eight(i, carry):
        for j in range(8):
            do(i, j)
        return carry

    lax.fori_loop(0, count // 8, eight, 0)


def forward_row(block, source, places, lookup, ghost=False):
    half = low_half((NV, 128))
    last = jnp.zeros_like(source) if ghost else -source
    if places is None:
        lhs = jnp.concatenate([jnp.zeros_like(source), jnp.where(half, 0.0, last)], axis=1)
    else:
        x0, x1, x2 = [lookup[i] for i in places]
        lhs = jnp.concatenate([jnp.where(half, x0, x1), jnp.where(half, x2, last)], axis=1)
    hi, lo = split(lhs)
    out = nt(jnp.concatenate([hi, lo], axis=0), block)
    out = out[:NV] + out[NV:]
    out = out + other_half(out)
    return source - out if ghost else -out


def clear(accs, window):
    for acc in accs:
        acc[pl.ds(0, window)] = jnp.zeros((window, NV, 128), F32)


def backward_row(block, value, places, accs):
    hi, lo = split(value)
    out = nn(jnp.concatenate([hi, lo], axis=0), block)
    out = out[:NV] + out[NV:]
    accs[0][places[0]] += out[:, :128]
    accs[1][places[1]] += out[:, :128]
    accs[2][places[2]] += out[:, 128:]
    return out[:, 128:]


def collected(accs, window):
    acc0, acc1, acc2 = [acc[pl.ds(0, window)] for acc in accs]
    total = jnp.where(low_half((window, NV, 128)), acc0 + acc2, acc1)
    return total + other_half(total)


def step_kernel(step, s_ref, w_ref, r_ref, a_ref, own_ref, near_ref, far_ref, res_ref, *refs):
    *outs, ext, acc0, acc1, acc2 = refs
    section = lax.axis_index("lvl")
    rnd, t = divmod(step, LV)
    first, handed = step == 0, t == 0

    def incoming(do):
        if handed:
            do(near_ref, far_ref)
        else:
            by_side(near_ref, far_ref, do)

    def outgoing(to_left, to_right, own):
        def put(near, far):
            if len(outs) == 1:
                outs[0][0] = near
                outs[0][1] = far
            else:
                outs[1][...] = near
                outs[2][...] = far

        if len(outs) == 3:
            outs[0][...] = own
        if len(outs) == 3 and t == LV - 1:
            put(to_left, to_right)
        else:
            even = is_even()
            pl.when(even)(lambda: put(to_right, to_left))
            pl.when(jnp.logical_not(even))(lambda: put(to_left, to_right))

    @pl.when(section == rnd)
    def _():
        if not first:
            ext[pl.ds(W, RL)] = unpack(own_ref[...])

            def fill(from_left, from_right):
                ext[pl.ds(0, W)] = unpack(from_left[...])
                ext[pl.ds(W + RL, W)] = unpack(from_right[...])

            incoming(fill)

        def one(i, j):
            q = i * 8 + j
            places = None if first else [s_ref[k * LV + t, q] for k in range(K)]
            res_ref[q] = forward_row(w_ref[q], r_ref[q], places, ext)

        in_eights(RL, one)
        x = res_ref[...]
        if len(outs) == 1:
            outgoing(pack(x), pack(x), None)
        else:
            outgoing(pack(x[:W]), pack(x[W:]), pack(x))

    @pl.when(section == LV - 1 - rnd)
    def _():
        level = LV - 1 - t
        if not first:
            ext[pl.ds(0, RL)] = unpack(own_ref[...])

            def add(from_left, from_right):
                ext[pl.ds(0, W)] += unpack(from_left[...])
                ext[pl.ds(W, W)] += unpack(from_right[...])

            incoming(add)
        accs = (acc0, acc1, acc2)
        clear(accs, EXT)

        def one(i, j):
            q = i * 8 + j
            value = a_ref[q] if first else a_ref[q] - ext[q]
            res_ref[q] = backward_row(w_ref[q], value, [s_ref[k * LV + level, q] for k in range(K)], accs)

        in_eights(RL, one)
        total = collected(accs, EXT)
        if len(outs) == 1:
            outgoing(pack(total[:RL]), pack(total[RL:]), None)
        else:
            outgoing(pack(total[:W]), pack(total[W + RL:]), pack(total[W:W + RL]))


def pair_kernel(rnd, t, s_ref, ghost_s, w0_ref, w1_ref, r0_ref, r1_ref, a0_ref, a1_ref, g_ref, gs_ref,
                own_near, own_far, near_ref, far_ref, res0_ref, res1_ref, *refs):
    *outs, ext, ext2, acc0, acc1, acc2 = refs
    section = lax.axis_index("lvl")

    def outgoing(to_left, to_right):
        def put(near, far):
            if len(outs) == 1:
                outs[0][0] = near
                outs[0][1] = far
            else:
                outs[0][...] = near
                outs[1][...] = far

        even = is_even()
        pl.when(even)(lambda: put(to_right, to_left))
        pl.when(jnp.logical_not(even))(lambda: put(to_left, to_right))

    def own_places(level, q, shift):
        return [s_ref[k * LV + level, q] + shift for k in range(K)]

    def ghost_places(ghost):
        return [ghost_s[k, ghost] for k in range(K)]

    @pl.when(section == rnd)
    def _():
        ext[pl.ds(RL, RL)] = unpack(own_near[...])

        def fill(from_left, from_right):
            ext[pl.ds(0, RL)] = unpack(from_left[...])
            ext[pl.ds(2 * RL, RL)] = unpack(from_right[...])

        by_side(near_ref, far_ref, fill)

        def ghost_row(i, j):
            ghost = i * 8 + j
            ext2[i * (W + RL) + j] = forward_row(g_ref[ghost], gs_ref[ghost], ghost_places(ghost), ext, True)

        def first_row(i, j):
            q = i * 8 + j
            x = forward_row(w0_ref[q], r0_ref[q], own_places(t, q, W), ext)
            ext2[W + q] = x
            res0_ref[q] = x

        def second_row(i, j):
            q = i * 8 + j
            res1_ref[q] = forward_row(w1_ref[q], r1_ref[q], own_places(t + 1, q, 0), ext2)

        in_eights(2 * W, ghost_row)
        in_eights(RL, first_row)
        in_eights(RL, second_row)
        x = res1_ref[...]
        outgoing(pack(x), pack(x))

    @pl.when(section == LV - 1 - rnd)
    def _():
        level = LV - 1 - t

        def gather(own_left, own_right):
            ext[pl.ds(0, RL)] = unpack(own_left[...])
            ext[pl.ds(RL, RL)] = unpack(own_right[...])

        def add(from_left, from_right):
            ext[pl.ds(0, RL)] += unpack(from_left[...])
            ext[pl.ds(RL, RL)] += unpack(from_right[...])

        by_side(own_near, own_far, gather)
        by_side(near_ref, far_ref, add)
        accs = (acc0, acc1, acc2)
        clear(accs, EXT + RL)

        def ghost_row(i, j):
            ghost = i * 8 + j
            backward_row(g_ref[ghost], gs_ref[ghost] - ext[i * (W + RL) + j], ghost_places(ghost), accs)

        def first_row(i, j):
            q = i * 8 + j
            res0_ref[q] = backward_row(w0_ref[q], a0_ref[q] - ext[W + q], own_places(level, q, W), accs)

        in_eights(2 * W, ghost_row)
        in_eights(RL, first_row)
        ext2[pl.ds(0, RL)] = collected(accs, EXT + RL)[RL:2 * RL]
        clear(accs, EXT)

        def second_row(i, j):
            q = i * 8 + j
            res1_ref[q] = backward_row(w1_ref[q], a1_ref[q] - ext2[q], own_places(level - 1, q, 0), accs)

        in_eights(RL, second_row)
        total = collected(accs, EXT)
        outgoing(pack(total[:RL]), pack(total[RL:]))


def ghost_send_kernel(part, s_ref, w_ref, r_ref, a_ref, near_ref, far_ref):
    forward = lax.axis_index("lvl") >= LV // 2
    shift = jnp.where(is_even(), W, 0)
    sub = lax.broadcasted_iota(jnp.int32, (8, 128), 0)
    left = low_half((B // 2, 128))
    left8 = low_half((8, 128))
    level = storage_level(part)
    for out_ref, base in ((near_ref, shift), (far_ref, W - shift)):

        def one(i, carry):
            block = w_ref[base + i]
            block = block[:B].astype(F32) + block[B:].astype(F32)
            out_ref[i, pl.ds(0, B), :] = block[:, :128]
            third = block[:, 128:]
            out_ref[i, pl.ds(B, B // 2), :] = jnp.where(left, third[:B // 2], other_half(third[B // 2:]))
            direct = forward_row(w_ref[base + i], r_ref[base + i], None, None)
            value = jnp.where(forward, direct, a_ref[base + i])
            out_ref[i, pl.ds(96, 8), :] = jnp.where(left8, value[:8], value[8:])
            places = jnp.zeros((8, 128), F32)
            for k in range(K):
                place = s_ref[k * LV + level, base + i].astype(F32)
                places = jnp.where(sub == k, place, places)
            out_ref[i, pl.ds(104, 8), :] = places
            return carry

        lax.fori_loop(0, W, one, 0, unroll=2)


def ghost_receive_kernel(near_ref, far_ref, g_ref, gs_ref, t_ref, table, sem):
    shift = jnp.where(is_even(), W, 0)
    lane = lax.broadcasted_iota(jnp.int32, (8, 128), 1)
    left = low_half((B // 2, 128))
    places = jnp.zeros((8, 128), F32)
    for in_ref, base in ((near_ref, shift), (far_ref, W - shift)):

        def one(i, places):
            first = in_ref[i, pl.ds(0, B), :]
            packed = in_ref[i, pl.ds(B, B // 2), :]
            third = jnp.concatenate(
                [jnp.where(left, packed, 0.0), jnp.where(left, other_half(packed), 0.0)], axis=0)
            hi, lo = split(jnp.concatenate([first, third], axis=1))
            g_ref[base + i] = jnp.concatenate([hi, lo], axis=0)
            gs_ref[base + i] = unpack(in_ref[i, pl.ds(96, 8), :].reshape(1, 8, 128)).reshape(NV, 128)
            return jnp.where(lane == base + i, in_ref[i, pl.ds(104, 8), :], places)

        places = lax.fori_loop(0, W, one, places, unroll=2)
    places = places.astype(jnp.int32) + jnp.where(lane < W, -W, RL + W)
    table[pl.ds(0, 8), :] = jnp.clip(places, 0, EXT + RL - 1)
    table[pl.ds(8, 8), :] = jnp.zeros((8, 128), jnp.int32)
    copy = pltpu.make_async_copy(table, t_ref, sem)
    copy.start()
    copy.wait()


def rows_kernel(rnd, levels, *refs):
    *refs, sol_ref, adj_ref, spread_ref, lines = refs
    results = refs[:len(levels)]
    section = lax.axis_index("lvl")
    forward = section == rnd

    @pl.when(jnp.logical_or(forward, section == LV - 1 - rnd))
    def _():
        spread = jnp.where(low_half((B * NV, 128)), 0.0, spread_matrix().astype(F32)).astype(BF16)
        spread_ref[...] = spread.reshape(B * NV // 128, 128, 128)
        mask = own_lane(RL * NV)
        for t, x in zip(levels, results):
            hi, lo = split(x[...].reshape(RL * NV, 128))

            def one(chunk, carry):
                part = spread_ref[chunk]
                wide = jnp.where(mask, nt(hi, part) + nt(lo, part), 0.0)
                lines[chunk] = jnp.sum(wide.reshape(RL, NV, 128), axis=1)
                return carry

            lax.fori_loop(0, B * NV // 128, one, 0, unroll=8 if rnd == LV - 1 and levels[0] else 1)
            for chunk in range(B * NV // 128):
                lanes = pl.ds(chunk * 128, 128)

                @pl.when(forward)
                def _():
                    sol_ref[t, :, lanes] = lines[chunk]

                @pl.when(jnp.logical_not(forward))
                def _():
                    adj_ref[LV - 1 - t, :, lanes] = lines[chunk]


def vspec():
    return pl.BlockSpec(memory_space=VMEM)


def sspec():
    return pl.BlockSpec(memory_space=SMEM)


def hspec():
    return pl.BlockSpec(memory_space=pl.ANY)


STATE = (RL, NV, 128)
OWN = (RL // 2, NV, 128)
SIDE = (W // 2, NV, 128)
MSGS = (2, RL // 2, NV, 128)
GHOST = (W, 112, 128)
GHOST_STEPS = {1: 3, 2: 1}
TABLE = ((K + 1) * LV, 128)
BLOCKS = (RL, 2 * B, 256)
SMEM_TABLE = SMEM(TABLE, jnp.int32)
OUT = (LV, RL, B * NV)


def params(mib):
    return pltpu.CompilerParams(vmem_limit_bytes=mib * MIB)


def cost(us):
    return pl.CostEstimate(flops=int(us * 1e9), bytes_accessed=int(us * 3e6), transcendentals=0)


def relay(owned, columns, owner):
    sent = (ROWS, B * NV // 128, 128)
    return pl.pallas_call(
        relay_kernel,
        out_shape=(pltpu.HBM(sent, F32), SMEM_TABLE),
        in_specs=[hspec()] * 3,
        out_specs=(hspec(), sspec()),
        scratch_shapes=[
            VMEM(TABLE, jnp.int32),
            VMEM((ROWS // 8, B * NV // 16, 128), F32),
            VMEM(owned.shape, F32),
            VMEM(columns.shape, jnp.int32),
            VMEM(owner.shape, jnp.int32),
            VMEM(sent, F32),
            pltpu.SemaphoreType.DMA((5,)),
        ],
        compiler_params=params(8),
        cost_estimate=cost(2.0),
        name="relay",
    )(in_hbm(owned), in_hbm(columns), in_hbm(owner))


def prepare(part, lower, dinv, rhs):
    wide = VMEM((RL * NV, B * NV), BF16)
    scratch = [
        VMEM((K, RL, B * B), F32),
        VMEM((RL, B * B), F32),
        VMEM((2, K + 1, 8 * B * B // 128, 128), F32),
        VMEM((4, 2, B, 128), F32),
        pltpu.SemaphoreType.DMA((3,)),
        wide,
        wide,
        VMEM((RL, B * NV), F32),
        VMEM((2, B * NV // 16, 128), F32),
    ]
    shapes = [VMEM(BLOCKS, BF16), VMEM(STATE, F32)]
    specs = [hspec(), hspec(), hspec()]
    return pl.pallas_call(
        partial(blocks_kernel, part),
        out_shape=shapes,
        in_specs=specs,
        out_specs=[vspec()] * len(shapes),
        scratch_shapes=scratch,
        compiler_params=params(12),
        cost_estimate=cost(2.5),
        name="prepare%d" % part,
    )(in_hbm(lower), in_hbm(dinv), in_hbm(rhs))


def adjoint_state(parts, table, relayed):
    wide = VMEM((RL * NV, B * NV), BF16)
    return call(partial(adjoint_kernel, parts), "adjoint_state", 0.6 * len(parts), [table, relayed],
                [VMEM(STATE, F32)] * len(parts), [wide, wide])


def call(body, name, us, kernel_args, shapes, scratch=(), mib=8, **more):
    def place(x):
        return in_smem(x) if x.dtype == jnp.int32 and x.shape == TABLE else in_vmem(x)

    def spec(x):
        return sspec() if x.dtype == jnp.int32 and x.shape == TABLE else vspec()

    return pl.pallas_call(
        body,
        out_shape=tuple(shapes),
        in_specs=[spec(x) for x in kernel_args],
        out_specs=tuple(sspec() if isinstance(x, type(SMEM_TABLE)) and x.memory_space == SMEM else vspec() for x in shapes),
        scratch_shapes=list(scratch),
        compiler_params=params(mib),
        cost_estimate=cost(us),
        name=name,
        **more,
    )(*[place(x) for x in kernel_args])


def run_step(step, table, blocks, source, adjoint, own, near, far):
    kernel_args = [table, blocks, source, adjoint]
    if own is not None:
        kernel_args += [own, near, far]

    def body(*refs):
        head, refs = refs[:4], refs[4:]
        arrivals = [None] * 3
        if own is not None:
            arrivals, refs = refs[:3], refs[3:]
        step_kernel(step, *head, *arrivals, *refs)

    shapes = [VMEM(STATE, F32)]
    shapes += [VMEM(MSGS, F32)] if step == 2 * LV - 1 else [VMEM(OWN, F32), VMEM(SIDE, F32), VMEM(SIDE, F32)]
    return call(body, "step%d" % step, 0.6, kernel_args, shapes, [VMEM((EXT, NV, 128), F32)] * 4)


def run_pair(rnd, t, table, blocks, source, adjoint, ghost, arrivals):
    kernel_args = [table, ghost[-1], *blocks, *source, *adjoint, *ghost[:-1], *arrivals]
    shapes = [VMEM(STATE, F32)] * 2
    shapes += [VMEM(OWN, F32)] * 2 if t == 0 else [VMEM(MSGS, F32)]

    scratch = [VMEM((EXT + RL, NV, 128), F32), VMEM((EXT, NV, 128), F32)] + [VMEM((EXT + RL, NV, 128), F32)] * 3
    return call(partial(pair_kernel, rnd, t), "pair%d_%d" % (rnd, t), 1.8, kernel_args, shapes, scratch)


def ghost_send(part, table, blocks, source, adjoint):
    return call(partial(ghost_send_kernel, part), "ghost_send", 0.5,
                [table, blocks, source, adjoint], [VMEM(GHOST, F32)] * 2)


def ghost_receive(near, far):
    return call(ghost_receive_kernel, "ghost_receive", 0.5, [near, far],
                [VMEM(BLOCKS, BF16), VMEM(STATE, F32), SMEM_TABLE],
                [VMEM(TABLE, jnp.int32), pltpu.SemaphoreType.DMA])


def to_rows(rnd, levels, results, outs):
    outs = [] if outs is None else list(outs)
    place = len(results)
    return call(partial(rows_kernel, rnd, levels), "rows%d_%d" % (rnd, levels[0]), 0.6 * len(levels),
                [*results, *outs], [VMEM(OUT, F32)] * 2,
                [VMEM((B * NV // 128, 128, 128), BF16), VMEM((B * NV // 128, RL, 128), F32)],
                input_output_aliases={place: 0, place + 1: 1} if outs else {})


def after(values, done):
    return lax.optimization_barrier((values, done))[0]


def per_device(rhs, adjoint_owned, owner_of, columns, lower, dinv):
    cells = lax.axis_size("cell")
    sections = lax.axis_size("lvl")
    lower = jnp.transpose(lower, (0, 2, 1, 3))
    columns = jnp.transpose(columns, (2, 0, 1))
    blocks, source, adjoint = ([None] * LV for _ in range(3))
    sent, table = relay(adjoint_owned, columns, owner_of)
    relayed = lax.all_to_all(sent.reshape(1, cells, B * NV), "cell", split_axis=1, concat_axis=1, tiled=True)
    relayed = relayed.reshape(ROWS, B * NV // 128, 128)
    for part in range(LV):
        blocks[part], source[part] = prepare(part, *after((lower, dinv, rhs), sent))
    adjoint[0], = adjoint_state((0,), table, relayed)

    near_of = [i ^ 1 for i in range(cells)]
    far_of = [(i + 1 if i % 2 else i - 1) % cells for i in range(cells)]

    def exchange(near, far):
        far_in = lax.ppermute(far, "cell", list(enumerate(far_of)))
        near_in = lax.ppermute(near, "cell", list(enumerate(near_of)))
        return near_in, far_in

    def shift_handoff(x, by):
        moves = [(0, 1), (sections - 1, sections - 2)]
        pairs = [(a * cells + i, b * cells + (i + by) % cells) for a, b in moves for i in range(cells)]
        return lax.ppermute(x, ("lvl", "cell"), pairs)

    def handoff(msgs, rnd):
        partner = [1, 0, 3, 2] if rnd % 2 == 0 else [3, 2, 1, 0]
        pairs = [(s * cells + i, partner[s] * cells + i) for s in range(sections) for i in range(cells)]
        return lax.ppermute(msgs, ("lvl", "cell"), pairs)

    ghosts = {}
    own = near = far = outs = None
    for step in range(2 * LV):
        rnd, t = divmod(step, LV)
        result, *sent_out = run_step(step, table, blocks[t], source[t], adjoint[t], own, near, far)
        if step == 0:
            adjoint[1:] = adjoint_state((1, 2, 3), table, after(relayed, sent_out[-1]))
        if step in GHOST_STEPS:
            part = GHOST_STEPS[step]
            shared = after((blocks[part], source[part], adjoint[part]), sent_out[-1])
            ghosts[part] = ghost_receive(*exchange(*ghost_send(part, table, *shared)))
        if t < LV - 1:
            own = sent_out[0]
            near, far = exchange(*sent_out[1:])
        elif rnd == 0:
            own, to_left, to_right = sent_out
            own, near, far = shift_handoff(own, 0), shift_handoff(to_right, 1), shift_handoff(to_left, -1)
        results = [result] if t == 0 else [*results, result]
        if t == LV - 1:
            outs = to_rows(rnd, tuple(range(LV)), results, outs)
    msgs = sent_out[0]
    for rnd in range(LV // 2, sections):
        msgs = handoff(msgs, rnd - 1)
        own_near, own_far = msgs[0], msgs[1]
        for t in (0, 2):
            parts = (LV - 1 - t, LV - 2 - t)
            arrivals = (own_near, own_far, *exchange(own_near, own_far))
            picked = [[x[p] for p in parts] for x in (blocks, source, adjoint)]
            first, second, *sent_out = run_pair(rnd, t, table, *picked, ghosts[parts[0]], arrivals)
            if t == 0:
                own_near, own_far = sent_out
            outs = to_rows(rnd, (t, t + 1), (first, second), outs)
        msgs = sent_out[0]
    return outs


def solution(mesh):
    return jax.shard_map(
        per_device,
        mesh=mesh,
        in_specs=(
            P("lvl", "cell", None),
            P("lvl", "cell", None),
            P("lvl", "cell"),
            P("lvl", "cell", None),
            P("lvl", "cell", None, None),
            P("lvl", "cell", None),
        ),
        out_specs=(P("lvl", "cell", None), P("lvl", "cell", None)),
        check_vma=False,
    )
```

profile of v0, /device:TPU:24, one launch (start us, length us, event | category | flops | bytes accessed | tf_op | source)
XLA Modules:
  0.0 136.4 jit_solution(5168154840113546558)
XLA Ops:
  2.4 11.9 %all-to-all-start = ((f32[1,64,1024]{2,0,1:T(1,128)}), f32[1,64,1024]{2,0,1:T(1,128)S(1)}, u32[]{:S(2)}, u32[]{:S(2)}) async-start(f32[1,64,1024]{2,0,1:T(1,128)} %bitcast.14), calls=%async_computation | async-start | bytes 524288 | tf_op jit(solution)/shard_map/all_to_all | solution.py:701
  14.4 4.9 %prepare0.1 = (bf16[16,128,256]{2,1,0:T(8,128)(2,1)S(1)}, f32[16,16,128]{2,1,0:T(8,128)S(1)}) custom-call(f32[4,3,16,4096]{3,2,1,0:T(8,128)} %bitcast.15, f32[4,16,4096]{2,1,0:T(8,128)} %dinv_hbm.3, f32[4,16,1024]{2,1,0:T(8,128)} %rhs_hbm.3), custom_call_target="tpu_custom_call" | custom-call | flops 2500000000 | bytes 7500000 | tf_op jit(solution)/shard_map/prepare0/pallas_call | solution.py:606
  19.3 4.9 %prepare1.1 = (bf16[16,128,256]{2,1,0:T(8,128)(2,1)S(1)}, f32[16,16,128]{2,1,0:T(8,128)S(1)}) custom-call(f32[4,3,16,4096]{3,2,1,0:T(8,128)} %bitcast.16, f32[4,16,4096]{2,1,0:T(8,128)} %dinv_hbm.3, f32[4,16,1024]{2,1,0:T(8,128)} %rhs_hbm.3), custom_call_target="tpu_custom_call" | custom-call | flops 2500000000 | bytes 7500000 | tf_op jit(solution)/shard_map/prepare1/pallas_call | solution.py:606
  24.2 2.1 %all-to-all-done = f32[1,64,1024]{2,0,1:T(1,128)S(1)} async-done(((f32[1,64,1024]{2,0,1:T(1,128)}), f32[1,64,1024]{2,0,1:T(1,128)S(1)}, u32[]{:S(2)}, u32[]{:S(2)}) %all-to-all-start) | async-done | bytes 262176 | tf_op jit(solution)/shard_map/all_to_all | solution.py:701
  28.2 2.9 %collective-permute-start.1 = (f32[4,16,128]{2,1,0:T(8,128)S(1)}, f32[4,16,128]{2,1,0:T(8,128)S(1)}, u32[]{:S(2)}, u32[]{:S(2)}) collective-permute-start(f32[4,16,128]{2,1,0:T(8,128)S(1)} %get-tuple-element.97), channel_id=1, source_target_pairs={{0,63},{1,2},{2,1},{3,4},{4,3},{5,6},{6,5},{7,8},{8,7},{9,10},{10,... | collective-permute-start | bytes 98312 | tf_op jit(solution)/shard_map/ppermute | solution.py:711
  31.1 3.5 %adjoint_state.3 = (f32[16,16,128]{2,1,0:T(8,128)S(1)}, f32[16,16,128]{2,1,0:T(8,128)S(1)}, f32[16,16,128]{2,1,0:T(8,128)S(1)}) custom-call(s32[16,128]{1,0:T(8,128)S(4)} %get-tuple-element.88.s_ref.refs_0_, f32[64,8,128]{2,1,0:T(8,128)S(1)} %bitcast.13), custom_call_target="tpu_custom_call" | custom-call | flops 1800000000 | bytes 5399999 | tf_op jit(solution)/shard_map/adjoint_state/pallas_call | solution.py:631
  36.1 2.7 %collective-permute-start.3 = (f32[4,16,128]{2,1,0:T(8,128)S(1)}, f32[4,16,128]{2,1,0:T(8,128)S(1)}, u32[]{:S(2)}, u32[]{:S(2)}) collective-permute-start(f32[4,16,128]{2,1,0:T(8,128)S(1)} %get-tuple-element.107), channel_id=1, source_target_pairs={{0,63},{1,2},{2,1},{3,4},{4,3},{5,6},{6,5},{7,8},{8,7},{9,10},{10,... | collective-permute-start | bytes 98312 | tf_op jit(solution)/shard_map/ppermute | solution.py:711
  38.8 4.9 %prepare2.1 = (bf16[16,128,256]{2,1,0:T(8,128)(2,1)S(1)}, f32[16,16,128]{2,1,0:T(8,128)S(1)}) custom-call(f32[4,3,16,4096]{3,2,1,0:T(8,128)} %bitcast.17, f32[4,16,4096]{2,1,0:T(8,128)} %dinv_hbm.3, f32[4,16,1024]{2,1,0:T(8,128)} %rhs_hbm.3), custom_call_target="tpu_custom_call" | custom-call | flops 2500000000 | bytes 7500000 | tf_op jit(solution)/shard_map/prepare2/pallas_call | solution.py:606
  44.6 2.5 %collective-permute-start.9 = (f32[4,16,128]{2,1,0:T(8,128)S(1)}, f32[4,16,128]{2,1,0:T(8,128)S(1)}, u32[]{:S(2)}, u32[]{:S(2)}) collective-permute-start(f32[4,16,128]{2,1,0:T(8,128)S(1)} %get-tuple-element.108), channel_id=1, source_target_pairs={{0,63},{1,2},{2,1},{3,4},{4,3},{5,6},{6,5},{7,8},{8,7},{9,10},{10,... | collective-permute-start | bytes 98312 | tf_op jit(solution)/shard_map/ppermute | solution.py:711
  47.1 4.9 %prepare3.1 = (bf16[16,128,256]{2,1,0:T(8,128)(2,1)S(1)}, f32[16,16,128]{2,1,0:T(8,128)S(1)}) custom-call(f32[4,3,16,4096]{3,2,1,0:T(8,128)} %bitcast.18, f32[4,16,4096]{2,1,0:T(8,128)} %dinv_hbm.3, f32[4,16,1024]{2,1,0:T(8,128)} %rhs_hbm.3), custom_call_target="tpu_custom_call" | custom-call | flops 2500000000 | bytes 7500000 | tf_op jit(solution)/shard_map/prepare3/pallas_call | solution.py:606
  60.6 4.7 %collective-permute-done.14.refs_6_ = f32[4,16,128]{2,1,0:T(8,128)S(1)} collective-permute-done((f32[4,16,128]{2,1,0:T(8,128)S(1)}, f32[4,16,128]{2,1,0:T(8,128)S(1)}, u32[]{:S(2)}, u32[]{:S(2)}) %collective-permute-start.14) | collective-permute-done | bytes 32800 | tf_op jit(solution)/shard_map/ppermute | solution.py:711
  67.3 4.7 %collective-permute-done.16.refs_6_ = f32[4,16,128]{2,1,0:T(8,128)S(1)} collective-permute-done((f32[4,16,128]{2,1,0:T(8,128)S(1)}, f32[4,16,128]{2,1,0:T(8,128)S(1)}, u32[]{:S(2)}, u32[]{:S(2)}) %collective-permute-start.16) | collective-permute-done | bytes 32800 | tf_op jit(solution)/shard_map/ppermute | solution.py:711
  75.9 3.2 %collective-permute-start.7 = (f32[8,112,128]{2,1,0:T(8,128)S(1)}, f32[8,112,128]{2,1,0:T(8,128)S(1)}, u32[]{:S(2)}, u32[]{:S(2)}) collective-permute-start(f32[8,112,128]{2,1,0:T(8,128)S(1)} %get-tuple-element.124), channel_id=1, source_target_pairs={{0,63},{1,2},{2,1},{3,4},{4,3},{5,6},{6,5},{7,8},{8,7},{9,10},{10,... | collective-permute-start | bytes 1376264 | tf_op jit(solution)/shard_map/ppermute | solution.py:711
  80.1 5.1 %collective-permute-done.19 = f32[2,8,16,128]{3,2,1,0:T(8,128)S(1)} collective-permute-done((f32[2,8,16,128]{3,2,1,0:T(8,128)S(1)}, f32[2,8,16,128]{3,2,1,0:T(8,128)S(1)}, u32[]{:S(2)}, u32[]{:S(2)}) %collective-permute-start.19) | collective-permute-done | bytes 131104 | tf_op jit(solution)/shard_map/ppermute | solution.py:723
  89.0 3.8 %collective-permute-start.5 = (f32[8,112,128]{2,1,0:T(8,128)S(1)}, f32[8,112,128]{2,1,0:T(8,128)S(1)}, u32[]{:S(2)}, u32[]{:S(2)}) collective-permute-start(f32[8,112,128]{2,1,0:T(8,128)S(1)} %get-tuple-element.113), channel_id=1, source_target_pairs={{0,63},{1,2},{2,1},{3,4},{4,3},{5,6},{6,5},{7,8},{8,7},{9,10},{10,... | collective-permute-start | bytes 1376264 | tf_op jit(solution)/shard_map/ppermute | solution.py:711
  95.7 6.7 %rows0_0.1 = (f32[4,16,1024]{2,1,0:T(8,128)S(1)}, f32[4,16,1024]{2,1,0:T(8,128)S(1)}) custom-call(f32[16,16,128]{2,1,0:T(8,128)S(1)} %get-tuple-element.160.refs_0_, f32[16,16,128]{2,1,0:T(8,128)S(1)} %get-tuple-element.161.refs_1_, f32[16,16,128]{2,1,0:T(8,128)S(1)} %get-tuple-element.162.refs_2_, f32[16,16,128]{2,1,0:T(8,128)S(1)} %get-tuple-element.163.refs_3_), custom_call_target="tpu_custom_call" | custom-call | flops 2400000000 | bytes 7200000 | tf_op jit(solution)/shard_map/rows0_0/pallas_call | solution.py:631
  103.8 7.6 %collective-permute-start.24 = (f32[2,8,16,128]{3,2,1,0:T(8,128)S(1)}, f32[2,8,16,128]{3,2,1,0:T(8,128)S(1)}, u32[]{:S(2)}, u32[]{:S(2)}) collective-permute-start(f32[2,8,16,128]{3,2,1,0:T(8,128)S(1)} %get-tuple-element.145), channel_id=1, source_target_pairs={{0,64},{1,65},{2,66},{3,67},{4,68},{5,69},{6,70},{7,71},{8,72},{9,... | collective-permute-start | bytes 393224 | tf_op jit(solution)/shard_map/ppermute | solution.py:723
  111.5 2.9 %collective-permute-done.24 = f32[2,8,16,128]{3,2,1,0:T(8,128)S(1)} collective-permute-done((f32[2,8,16,128]{3,2,1,0:T(8,128)S(1)}, f32[2,8,16,128]{3,2,1,0:T(8,128)S(1)}, u32[]{:S(2)}, u32[]{:S(2)}) %collective-permute-start.24) | collective-permute-done | bytes 131104 | tf_op jit(solution)/shard_map/ppermute | solution.py:723
  114.4 2.0 %collective-permute-start.26 = (f32[8,16,128]{2,1,0:T(8,128)S(1)}, f32[8,16,128]{2,1,0:T(8,128)S(1)}, u32[]{:S(2)}, u32[]{:S(2)}) collective-permute-start(f32[8,16,128]{2,1,0:T(8,128)S(1)} %get-tuple-element.174.own_far), channel_id=1, source_target_pairs={{0,63},{1,2},{2,1},{3,4},{4,3},{5,6},{6,5},{7,8},{8,7},{9,10},{10,... | collective-permute-start | bytes 196616 | tf_op jit(solution)/shard_map/ppermute | solution.py:711
  116.4 5.1 %collective-permute-done.26.far_ref = f32[8,16,128]{2,1,0:T(8,128)S(1)} collective-permute-done((f32[8,16,128]{2,1,0:T(8,128)S(1)}, f32[8,16,128]{2,1,0:T(8,128)S(1)}, u32[]{:S(2)}, u32[]{:S(2)}) %collective-permute-start.26) | collective-permute-done | bytes 65568 | tf_op jit(solution)/shard_map/ppermute | solution.py:711
  121.5 2.3 %pair3_0.1 = (f32[16,16,128]{2,1,0:T(8,128)S(1)}, f32[16,16,128]{2,1,0:T(8,128)S(1)}, f32[8,16,128]{2,1,0:T(8,128)S(1)}, f32[8,16,128]{2,1,0:T(8,128)S(1)}) custom-call(s32[16,128]{1,0:T(8,128)S(4)} %get-tuple-element.88.s_ref.refs_0_, s32[16,128]{1,0:T(8,128)S(4)} %get-tuple-element.125.ghost_s, ...), custom_call_target="tpu_custom_call" | custom-call | flops 1800000000 | bytes 5400000 | tf_op jit(solution)/shard_map/pair3_0/pallas_call | solution.py:631
  123.9 2.0 %collective-permute-start.28 = (f32[8,16,128]{2,1,0:T(8,128)S(1)}, f32[8,16,128]{2,1,0:T(8,128)S(1)}, u32[]{:S(2)}, u32[]{:S(2)}) collective-permute-start(f32[8,16,128]{2,1,0:T(8,128)S(1)} %get-tuple-element.147.own_far), channel_id=1, source_target_pairs={{0,63},{1,2},{2,1},{3,4},{4,3},{5,6},{6,5},{7,8},{8,7},{9,10},{10,... | collective-permute-start | bytes 196616 | tf_op jit(solution)/shard_map/ppermute | solution.py:711
  125.9 3.4 %rows3_0.1 = (f32[4,16,1024]{2,1,0:T(8,128)S(1)}, f32[4,16,1024]{2,1,0:T(8,128)S(1)}) custom-call(f32[16,16,128]{2,1,0:T(8,128)S(1)} %get-tuple-element.150.refs_0_, f32[16,16,128]{2,1,0:T(8,128)S(1)} %get-tuple-element.151.refs_1_, f32[4,16,1024]{2,1,0:T(8,128)S(1)} %get-tuple-element.170.refs_2_, ...), custom_call_target="tpu_custom_call", output_to_operand_aliasing={{0}: (2, {}), {1}: (3, {})} | custom-call | flops 1200000000 | bytes 3600000 | tf_op jit(solution)/shard_map/rows3_0/pallas_call | solution.py:631
  131.0 3.0 %pair3_2.1 = (f32[16,16,128]{2,1,0:T(8,128)S(1)}, f32[16,16,128]{2,1,0:T(8,128)S(1)}, f32[2,8,16,128]{3,2,1,0:T(8,128)}) custom-call(s32[16,128]{1,0:T(8,128)S(4)} %get-tuple-element.88.s_ref.refs_0_, s32[16,128]{1,0:T(8,128)S(4)} %get-tuple-element.114.ghost_s, bf16[16,128,256]{2,1,0:T(8,128)(2,1)S(1)} %get-tuple-element.109.refs_1_.w_ref.w0_ref, ...), custom_call_target="tpu_custom_call" | custom-call | flops 1800000000 | bytes 5400000 | tf_op jit(solution)/shard_map/pair3_2/pallas_call | solution.py:631
  (69 shorter events, 33.5 us)
Async XLA Ops:
  2.4 23.9 %all-to-all-start = ((f32[1,64,1024]{2,0,1:T(1,128)}), f32[1,64,1024]{2,0,1:T(1,128)S(1)}, u32[]{:S(2)}, u32[]{:S(2)}) async-start(f32[1,64,1024]{2,0,1:T(1,128)} %bitcast.14), calls=%async_computation | async-start | bytes 524288 | tf_op jit(solution)/shard_map/all_to_all | solution.py:701
  28.2 6.7 %collective-permute-start.1 = (f32[4,16,128]{2,1,0:T(8,128)S(1)}, f32[4,16,128]{2,1,0:T(8,128)S(1)}, u32[]{:S(2)}, u32[]{:S(2)}) collective-permute-start(f32[4,16,128]{2,1,0:T(8,128)S(1)} %get-tuple-element.97), channel_id=1, source_target_pairs={{0,63},{1,2},{2,1},{3,4},{4,3},{5,6},{6,5},{7,8},{8,7},{9,10},{10,... | collective-permute-start | bytes 98312 | tf_op jit(solution)/shard_map/ppermute | solution.py:711
  35.7 8.0 %collective-permute-start.2 = (f32[4,16,128]{2,1,0:T(8,128)S(1)}, f32[4,16,128]{2,1,0:T(8,128)S(1)}, u32[]{:S(2)}, u32[]{:S(2)}) collective-permute-start(f32[4,16,128]{2,1,0:T(8,128)S(1)} %get-tuple-element.106), channel_id=1, source_target_pairs={{0,1},{1,0},{2,3},{3,2},{4,5},{5,4},{6,7},{7,6},{8,9},{9,8},{10,11... | collective-permute-start | bytes 98312 | tf_op jit(solution)/shard_map/ppermute | solution.py:712
  36.1 7.6 %collective-permute-start.3 = (f32[4,16,128]{2,1,0:T(8,128)S(1)}, f32[4,16,128]{2,1,0:T(8,128)S(1)}, u32[]{:S(2)}, u32[]{:S(2)}) collective-permute-start(f32[4,16,128]{2,1,0:T(8,128)S(1)} %get-tuple-element.107), channel_id=1, source_target_pairs={{0,63},{1,2},{2,1},{3,4},{4,3},{5,6},{6,5},{7,8},{8,7},{9,10},{10,... | collective-permute-start | bytes 98312 | tf_op jit(solution)/shard_map/ppermute | solution.py:711
  44.5 7.5 %collective-permute-start.8 = (f32[4,16,128]{2,1,0:T(8,128)S(1)}, f32[4,16,128]{2,1,0:T(8,128)S(1)}, u32[]{:S(2)}, u32[]{:S(2)}) collective-permute-start(f32[4,16,128]{2,1,0:T(8,128)S(1)} %get-tuple-element.129), channel_id=1, source_target_pairs={{0,1},{1,0},{2,3},{3,2},{4,5},{5,4},{6,7},{7,6},{8,9},{9,8},{10,11... | collective-permute-start | bytes 98312 | tf_op jit(solution)/shard_map/ppermute | solution.py:712
  44.6 7.4 %collective-permute-start.9 = (f32[4,16,128]{2,1,0:T(8,128)S(1)}, f32[4,16,128]{2,1,0:T(8,128)S(1)}, u32[]{:S(2)}, u32[]{:S(2)}) collective-permute-start(f32[4,16,128]{2,1,0:T(8,128)S(1)} %get-tuple-element.108), channel_id=1, source_target_pairs={{0,63},{1,2},{2,1},{3,4},{4,3},{5,6},{6,5},{7,8},{8,7},{9,10},{10,... | collective-permute-start | bytes 98312 | tf_op jit(solution)/shard_map/ppermute | solution.py:711
  52.9 5.8 %collective-permute-start.10 = (f32[8,16,128]{2,1,0:T(8,128)S(1)}, f32[8,16,128]{2,1,0:T(8,128)S(1)}, u32[]{:S(2)}, u32[]{:S(2)}) collective-permute-start(f32[8,16,128]{2,1,0:T(8,128)S(1)} %get-tuple-element.130), channel_id=1, source_target_pairs={{0,64},{1,65},{2,66},{3,67},{4,68},{5,69},{6,70},{7,71},{8,72},{9,... | collective-permute-start | bytes 196616 | tf_op jit(solution)/shard_map/ppermute | solution.py:718
  58.7 6.7 %collective-permute-start.14 = (f32[4,16,128]{2,1,0:T(8,128)S(1)}, f32[4,16,128]{2,1,0:T(8,128)S(1)}, u32[]{:S(2)}, u32[]{:S(2)}) collective-permute-start(f32[4,16,128]{2,1,0:T(8,128)S(1)} %get-tuple-element.135), channel_id=1, source_target_pairs={{0,63},{1,2},{2,1},{3,4},{4,3},{5,6},{6,5},{7,8},{8,7},{9,10},{10,... | collective-permute-start | bytes 98312 | tf_op jit(solution)/shard_map/ppermute | solution.py:711
  65.3 6.7 %collective-permute-start.16 = (f32[4,16,128]{2,1,0:T(8,128)S(1)}, f32[4,16,128]{2,1,0:T(8,128)S(1)}, u32[]{:S(2)}, u32[]{:S(2)}) collective-permute-start(f32[4,16,128]{2,1,0:T(8,128)S(1)} %get-tuple-element.138), channel_id=1, source_target_pairs={{0,63},{1,2},{2,1},{3,4},{4,3},{5,6},{6,5},{7,8},{8,7},{9,10},{10,... | collective-permute-start | bytes 98312 | tf_op jit(solution)/shard_map/ppermute | solution.py:711
  72.0 7.1 %collective-permute-start.17 = (f32[4,16,128]{2,1,0:T(8,128)S(1)}, f32[4,16,128]{2,1,0:T(8,128)S(1)}, u32[]{:S(2)}, u32[]{:S(2)}) collective-permute-start(f32[4,16,128]{2,1,0:T(8,128)S(1)} %get-tuple-element.140), channel_id=1, source_target_pairs={{0,1},{1,0},{2,3},{3,2},{4,5},{5,4},{6,7},{7,6},{8,9},{9,8},{10,11... | collective-permute-start | bytes 98312 | tf_op jit(solution)/shard_map/ppermute | solution.py:712
  72.0 7.1 %collective-permute-start.18 = (f32[4,16,128]{2,1,0:T(8,128)S(1)}, f32[4,16,128]{2,1,0:T(8,128)S(1)}, u32[]{:S(2)}, u32[]{:S(2)}) collective-permute-start(f32[4,16,128]{2,1,0:T(8,128)S(1)} %get-tuple-element.141), channel_id=1, source_target_pairs={{0,63},{1,2},{2,1},{3,4},{4,3},{5,6},{6,5},{7,8},{8,7},{9,10},{10,... | collective-permute-start | bytes 98312 | tf_op jit(solution)/shard_map/ppermute | solution.py:711
  75.8 13.2 %collective-permute-start.6 = (f32[8,112,128]{2,1,0:T(8,128)S(1)}, f32[8,112,128]{2,1,0:T(8,128)S(1)}, u32[]{:S(2)}, u32[]{:S(2)}) collective-permute-start(f32[8,112,128]{2,1,0:T(8,128)S(1)} %get-tuple-element.123), channel_id=1, source_target_pairs={{0,1},{1,0},{2,3},{3,2},{4,5},{5,4},{6,7},{7,6},{8,9},{9,8},{10,11... | collective-permute-start | bytes 1376264 | tf_op jit(solution)/shard_map/ppermute | solution.py:712
  75.9 17.0 %collective-permute-start.7 = (f32[8,112,128]{2,1,0:T(8,128)S(1)}, f32[8,112,128]{2,1,0:T(8,128)S(1)}, u32[]{:S(2)}, u32[]{:S(2)}) collective-permute-start(f32[8,112,128]{2,1,0:T(8,128)S(1)} %get-tuple-element.124), channel_id=1, source_target_pairs={{0,63},{1,2},{2,1},{3,4},{4,3},{5,6},{6,5},{7,8},{8,7},{9,10},{10,... | collective-permute-start | bytes 1376264 | tf_op jit(solution)/shard_map/ppermute | solution.py:711
  79.1 6.2 %collective-permute-start.19 = (f32[2,8,16,128]{3,2,1,0:T(8,128)S(1)}, f32[2,8,16,128]{3,2,1,0:T(8,128)S(1)}, u32[]{:S(2)}, u32[]{:S(2)}) collective-permute-start(f32[2,8,16,128]{3,2,1,0:T(8,128)S(1)} %get-tuple-element.142), channel_id=1, source_target_pairs={{0,192},{1,193},{2,194},{3,195},{4,196},{5,197},{6,198},{7,199},{8... | collective-permute-start | bytes 393224 | tf_op jit(solution)/shard_map/ppermute | solution.py:723
  85.3 8.9 %collective-permute-start.21 = (f32[8,16,128]{2,1,0:T(8,128)S(1)}, f32[8,16,128]{2,1,0:T(8,128)S(1)}, u32[]{:S(2)}, u32[]{:S(2)}) collective-permute-start(f32[8,16,128]{2,1,0:T(8,128)S(1)} %get-tuple-element.176.own_far), channel_id=1, source_target_pairs={{0,63},{1,2},{2,1},{3,4},{4,3},{5,6},{6,5},{7,8},{8,7},{9,10},{10,... | collective-permute-start | bytes 196616 | tf_op jit(solution)/shard_map/ppermute | solution.py:711
  86.6 7.6 %collective-permute-start.20 = (f32[8,16,128]{2,1,0:T(8,128)S(1)}, f32[8,16,128]{2,1,0:T(8,128)S(1)}, u32[]{:S(2)}, u32[]{:S(2)}) collective-permute-start(f32[8,16,128]{2,1,0:T(8,128)S(1)} %get-tuple-element.177.own_near), channel_id=1, source_target_pairs={{0,1},{1,0},{2,3},{3,2},{4,5},{5,4},{6,7},{7,6},{8,9},{9,8},{10,11... | collective-permute-start | bytes 196616 | tf_op jit(solution)/shard_map/ppermute | solution.py:712
  88.4 14.0 %collective-permute-start.4 = (f32[8,112,128]{2,1,0:T(8,128)S(1)}, f32[8,112,128]{2,1,0:T(8,128)S(1)}, u32[]{:S(2)}, u32[]{:S(2)}) collective-permute-start(f32[8,112,128]{2,1,0:T(8,128)S(1)} %get-tuple-element.112), channel_id=1, source_target_pairs={{0,1},{1,0},{2,3},{3,2},{4,5},{5,4},{6,7},{7,6},{8,9},{9,8},{10,11... | collective-permute-start | bytes 1376264 | tf_op jit(solution)/shard_map/ppermute | solution.py:712
  89.0 13.4 %collective-permute-start.5 = (f32[8,112,128]{2,1,0:T(8,128)S(1)}, f32[8,112,128]{2,1,0:T(8,128)S(1)}, u32[]{:S(2)}, u32[]{:S(2)}) collective-permute-start(f32[8,112,128]{2,1,0:T(8,128)S(1)} %get-tuple-element.113), channel_id=1, source_target_pairs={{0,63},{1,2},{2,1},{3,4},{4,3},{5,6},{6,5},{7,8},{8,7},{9,10},{10,... | collective-permute-start | bytes 1376264 | tf_op jit(solution)/shard_map/ppermute | solution.py:711
  94.2 9.6 %collective-permute-start.22 = (f32[8,16,128]{2,1,0:T(8,128)S(1)}, f32[8,16,128]{2,1,0:T(8,128)S(1)}, u32[]{:S(2)}, u32[]{:S(2)}) collective-permute-start(f32[8,16,128]{2,1,0:T(8,128)S(1)} %get-tuple-element.143.own_near), channel_id=1, source_target_pairs={{0,1},{1,0},{2,3},{3,2},{4,5},{5,4},{6,7},{7,6},{8,9},{9,8},{10,11... | collective-permute-start | bytes 196616 | tf_op jit(solution)/shard_map/ppermute | solution.py:712
  94.3 9.5 %collective-permute-start.23 = (f32[8,16,128]{2,1,0:T(8,128)S(1)}, f32[8,16,128]{2,1,0:T(8,128)S(1)}, u32[]{:S(2)}, u32[]{:S(2)}) collective-permute-start(f32[8,16,128]{2,1,0:T(8,128)S(1)} %get-tuple-element.144.own_far), channel_id=1, source_target_pairs={{0,63},{1,2},{2,1},{3,4},{4,3},{5,6},{6,5},{7,8},{8,7},{9,10},{10,... | collective-permute-start | bytes 196616 | tf_op jit(solution)/shard_map/ppermute | solution.py:711
  103.8 10.6 %collective-permute-start.24 = (f32[2,8,16,128]{3,2,1,0:T(8,128)S(1)}, f32[2,8,16,128]{3,2,1,0:T(8,128)S(1)}, u32[]{:S(2)}, u32[]{:S(2)}) collective-permute-start(f32[2,8,16,128]{3,2,1,0:T(8,128)S(1)} %get-tuple-element.145), channel_id=1, source_target_pairs={{0,64},{1,65},{2,66},{3,67},{4,68},{5,69},{6,70},{7,71},{8,72},{9,... | collective-permute-start | bytes 393224 | tf_op jit(solution)/shard_map/ppermute | solution.py:723
  114.4 7.1 %collective-permute-start.26 = (f32[8,16,128]{2,1,0:T(8,128)S(1)}, f32[8,16,128]{2,1,0:T(8,128)S(1)}, u32[]{:S(2)}, u32[]{:S(2)}) collective-permute-start(f32[8,16,128]{2,1,0:T(8,128)S(1)} %get-tuple-element.174.own_far), channel_id=1, source_target_pairs={{0,63},{1,2},{2,1},{3,4},{4,3},{5,6},{6,5},{7,8},{8,7},{9,10},{10,... | collective-permute-start | bytes 196616 | tf_op jit(solution)/shard_map/ppermute | solution.py:711
  123.8 5.5 %collective-permute-start.27 = (f32[8,16,128]{2,1,0:T(8,128)S(1)}, f32[8,16,128]{2,1,0:T(8,128)S(1)}, u32[]{:S(2)}, u32[]{:S(2)}) collective-permute-start(f32[8,16,128]{2,1,0:T(8,128)S(1)} %get-tuple-element.146.own_near), channel_id=1, source_target_pairs={{0,1},{1,0},{2,3},{3,2},{4,5},{5,4},{6,7},{7,6},{8,9},{9,8},{10,11... | collective-permute-start | bytes 196616 | tf_op jit(solution)/shard_map/ppermute | solution.py:712
  123.9 7.1 %collective-permute-start.28 = (f32[8,16,128]{2,1,0:T(8,128)S(1)}, f32[8,16,128]{2,1,0:T(8,128)S(1)}, u32[]{:S(2)}, u32[]{:S(2)}) collective-permute-start(f32[8,16,128]{2,1,0:T(8,128)S(1)} %get-tuple-element.147.own_far), channel_id=1, source_target_pairs={{0,63},{1,2},{2,1},{3,4},{4,3},{5,6},{6,5},{7,8},{8,7},{9,10},{10,... | collective-permute-start | bytes 196616 | tf_op jit(solution)/shard_map/ppermute | solution.py:711
  (6 other events, 18.7 us)
where the time goes:
time: 138 us; the launch traced here: 136 us
  starting transfers between devices  53.7 us (39%)
  Pallas kernels  52 us (38%)
  waiting for transfers between devices  28.3 us (21%)
  local copies, waits for them, and re-layouts  1.43 us (1%)
    pallas_call x24, Pallas kernels, call(): pl.pallas_call(body, out_shape=tuple(shapes), in_specs=[spec(x) for x in...  30.6 us
    ppermute x12, starting transfers between devices, exchange(): far_in = lax.ppermute(far, 'cell', list(enumerate(far_of)))  27.6 us
    pallas_call x4, Pallas kernels, prepare(): pl.pallas_call(partial(blocks_kernel, part), out_shape=shapes, in_specs=s...  19.7 us
    ppermute x12, waiting for transfers between devices, exchange(): far_in = lax.ppermute(far, 'cell', list(enumerate(far_of)))  16.5 us
    all_to_all x1, starting transfers between devices, per_device(): lax.all_to_all(sent.reshape(1, cells, B * NV), 'cell', split_axis=1, conc...  11.9 us
    ppermute x2, starting transfers between devices, handoff(): return lax.ppermute(msgs, ('lvl', 'cell'), pairs)  8.64 us
    ppermute x2, waiting for transfers between devices, handoff(): return lax.ppermute(msgs, ('lvl', 'cell'), pairs)  8.09 us
    ppermute x3, starting transfers between devices, shift_handoff(): return lax.ppermute(x, ('lvl', 'cell'), pairs)  4.2 us
  transfers between devices with their start and end apart: 30, of which 9 were waited for; matrix products, arithmetic and copies ran while one was open for 0% of the time, Pallas kernels for 29%

commit v1 on v0

--- a/solution.py
+++ b/solution.py
@@ -189,12 +189,12 @@
         hi, lo = split(jnp.concatenate([product[:, :128], tail], axis=1))
         w_ref[half * 8 + row] = jnp.concatenate([hi, lo], axis=0)
 
-    def two_rows(pair, carry):
-        for row in range(2):
-            row_blocks(pair // 4, pair % 4 * 2 + row, row)
+    def four_rows(pair, carry):
+        for row in range(4):
+            row_blocks(pair // 2, pair % 2 * 4 + row, row)
         return carry
 
-    lax.fori_loop(0, RL // 2, two_rows, 0)
+    lax.fori_loop(0, RL // 4, four_rows, 0)
 
 
 def adjoint_kernel(parts, s_ref, relayed_ref, *refs):
@@ -230,12 +230,9 @@
 
 
 def in_eights(count, do):
-    def eight(i, carry):
+    for i in range(count // 8):
         for j in range(8):
             do(i, j)
-        return carry
-
-    lax.fori_loop(0, count // 8, eight, 0)
 
 
 def forward_row(block, source, places, lookup, ghost=False):
@@ -472,7 +469,7 @@
             out_ref[i, pl.ds(104, 8), :] = places
             return carry
 
-        lax.fori_loop(0, W, one, 0, unroll=2)
+        lax.fori_loop(0, W, one, 0)
 
 
 def ghost_receive_kernel(near_ref, far_ref, g_ref, gs_ref, t_ref, table, sem):
@@ -492,7 +489,7 @@
             gs_ref[base + i] = unpack(in_ref[i, pl.ds(96, 8), :].reshape(1, 8, 128)).reshape(NV, 128)
             return jnp.where(lane == base + i, in_ref[i, pl.ds(104, 8), :], places)
 
-        places = lax.fori_loop(0, W, one, places, unroll=2)
+        places = lax.fori_loop(0, W, one, places)
     places = places.astype(jnp.int32) + jnp.where(lane < W, -W, RL + W)
     table[pl.ds(0, 8), :] = jnp.clip(places, 0, EXT + RL - 1)
     table[pl.ds(8, 8), :] = jnp.zeros((8, 128), jnp.int32)
@@ -502,7 +499,7 @@
 
 
 def rows_kernel(rnd, levels, *refs):
-    *refs, sol_ref, adj_ref, spread_ref, lines = refs
+    *refs, sol_ref, adj_ref, spread_ref = refs
     results = refs[:len(levels)]
     section = lax.axis_index("lvl")
     forward = section == rnd
@@ -518,20 +515,20 @@
             def one(chunk, carry):
                 part = spread_ref[chunk]
                 wide = jnp.where(mask, nt(hi, part) + nt(lo, part), 0.0)
-                lines[chunk] = jnp.sum(wide.reshape(RL, NV, 128), axis=1)
-                return carry
-
-            lax.fori_loop(0, B * NV // 128, one, 0, unroll=8 if rnd == LV - 1 and levels[0] else 1)
-            for chunk in range(B * NV // 128):
-                lanes = pl.ds(chunk * 128, 128)
+                value = jnp.sum(wide.reshape(RL, NV, 128), axis=1)
+                lanes = pl.ds(pl.multiple_of(chunk * 128, 128), 128)
 
                 @pl.when(forward)
                 def _():
-                    sol_ref[t, :, lanes] = lines[chunk]
+                    sol_ref[t, :, lanes] = value
 
                 @pl.when(jnp.logical_not(forward))
                 def _():
-                    adj_ref[LV - 1 - t, :, lanes] = lines[chunk]
+                    adj_ref[LV - 1 - t, :, lanes] = value
+
+                return carry
+
+            lax.fori_loop(0, B * NV // 128, one, 0, unroll=4 if rnd == LV - 1 and levels[0] else 1)
 
 
 def vspec():
@@ -683,7 +680,7 @@
     place = len(results)
     return call(partial(rows_kernel, rnd, levels), "rows%d_%d" % (rnd, levels[0]), 0.6 * len(levels),
                 [*results, *outs], [VMEM(OUT, F32)] * 2,
-                [VMEM((B * NV // 128, 128, 128), BF16), VMEM((B * NV // 128, RL, 128), F32)],
+                [VMEM((B * NV // 128, 128, 128), BF16)],
                 input_output_aliases={place: 0, place + 1: 1} if outs else {})
 
 

time: 138 us -> 137 us (level); the launches traced: 136 us -> 137 us
  starting transfers between devices: 53.7 us -> 49.1 us
  waiting for transfers between devices: 28.3 us -> 32.5 us
    pallas_call x24, Pallas kernels: 30.6 us -> 35.6 us  [call(): pl.pallas_call(body, out_shape=tuple(shapes), in_specs=[spec(x) for x in...]
    pallas_call x4, Pallas kernels: 19.7 us -> 15.7 us  [prepare(): pl.pallas_call(partial(blocks_kernel, part), out_shape=shapes, in_specs=s...]
    ppermute x2, starting transfers between devices: 8.64 us -> 5.75 us  [handoff(): return lax.ppermute(msgs, ('lvl', 'cell'), pairs)]
    ppermute x12, waiting for transfers between devices: 16.5 us -> 18.7 us  [exchange(): far_in = lax.ppermute(far, 'cell', list(enumerate(far_of)))]
    all_to_all x1, waiting for transfers between devices: 2.14 us -> 4.1 us  [per_device(): lax.all_to_all(sent.reshape(1, cells, B * NV), 'cell', split_axis=1, conc...]
    ppermute x12, starting transfers between devices: 27.6 us -> 25.8 us  [exchange(): far_in = lax.ppermute(far, 'cell', list(enumerate(far_of)))]
  transfers between devices with their start and end apart: 30 -> 30, of which waited for: 9 -> 11; matrix products, arithmetic and copies ran while one was open for 0% -> 0% of each run, Pallas kernels for 29% -> 29%
where the time goes in v1:
time: 137 us
  Pallas kernels  53.1 us (39%)
  starting transfers between devices  49.1 us (36%)
  waiting for transfers between devices  32.5 us (24%)
  local copies, waits for them, and re-layouts  1.43 us (1%)
    pallas_call x24, Pallas kernels, call(): pl.pallas_call(body, out_shape=tuple(shapes), in_specs=[spec(x) for x in...  35.6 us
    ppermute x12, starting transfers between devices, exchange(): far_in = lax.ppermute(far, 'cell', list(enumerate(far_of)))  25.8 us
    ppermute x12, waiting for transfers between devices, exchange(): far_in = lax.ppermute(far, 'cell', list(enumerate(far_of)))  18.7 us
    pallas_call x4, Pallas kernels, prepare(): pl.pallas_call(partial(blocks_kernel, part), out_shape=shapes, in_specs=s...  15.7 us
    all_to_all x1, starting transfers between devices, per_device(): lax.all_to_all(sent.reshape(1, cells, B * NV), 'cell', split_axis=1, conc...  11.9 us
    ppermute x2, waiting for transfers between devices, handoff(): return lax.ppermute(msgs, ('lvl', 'cell'), pairs)  8.08 us
    ppermute x2, starting transfers between devices, handoff(): return lax.ppermute(msgs, ('lvl', 'cell'), pairs)  5.75 us
    ppermute x3, starting transfers between devices, shift_handoff(): return lax.ppermute(x, ('lvl', 'cell'), pairs)  4.67 us
  transfers between devices with their start and end apart: 30, of which 11 were waited for; matrix products, arithmetic and copies ran while one was open for 0% of the time, Pallas kernels for 29%

profile of v1, /device:TPU:24, one launch (start us, length us, event | category | flops | bytes accessed | tf_op | source)
XLA Modules:
  0.0 137.1 jit_solution(14792796743098214320)
XLA Ops:
  2.4 11.9 %all-to-all-start = ((f32[1,64,1024]{2,0,1:T(1,128)}), f32[1,64,1024]{2,0,1:T(1,128)S(1)}, u32[]{:S(2)}, u32[]{:S(2)}) async-start(f32[1,64,1024]{2,0,1:T(1,128)} %bitcast.14), calls=%async_computation | async-start | bytes 524288 | tf_op jit(solution)/shard_map/all_to_all | solution.py:698
  14.4 3.9 %prepare0.1 = (bf16[16,128,256]{2,1,0:T(8,128)(2,1)S(1)}, f32[16,16,128]{2,1,0:T(8,128)S(1)}) custom-call(f32[4,3,16,4096]{3,2,1,0:T(8,128)} %bitcast.15, f32[4,16,4096]{2,1,0:T(8,128)} %dinv_hbm.3, f32[4,16,1024]{2,1,0:T(8,128)} %rhs_hbm.3), custom_call_target="tpu_custom_call" | custom-call | flops 2500000000 | bytes 7500000 | tf_op jit(solution)/shard_map/prepare0/pallas_call | solution.py:603
  18.3 3.9 %prepare1.1 = (bf16[16,128,256]{2,1,0:T(8,128)(2,1)S(1)}, f32[16,16,128]{2,1,0:T(8,128)S(1)}) custom-call(f32[4,3,16,4096]{3,2,1,0:T(8,128)} %bitcast.16, f32[4,16,4096]{2,1,0:T(8,128)} %dinv_hbm.3, f32[4,16,1024]{2,1,0:T(8,128)} %rhs_hbm.3), custom_call_target="tpu_custom_call" | custom-call | flops 2500000000 | bytes 7500000 | tf_op jit(solution)/shard_map/prepare1/pallas_call | solution.py:603
  22.3 4.1 %all-to-all-done = f32[1,64,1024]{2,0,1:T(1,128)S(1)} async-done(((f32[1,64,1024]{2,0,1:T(1,128)}), f32[1,64,1024]{2,0,1:T(1,128)S(1)}, u32[]{:S(2)}, u32[]{:S(2)}) %all-to-all-start) | async-done | bytes 262176 | tf_op jit(solution)/shard_map/all_to_all | solution.py:698
  29.6 3.5 %adjoint_state.3 = (f32[16,16,128]{2,1,0:T(8,128)S(1)}, f32[16,16,128]{2,1,0:T(8,128)S(1)}, f32[16,16,128]{2,1,0:T(8,128)S(1)}) custom-call(s32[16,128]{1,0:T(8,128)S(4)} %get-tuple-element.88.s_ref.refs_0_, f32[64,8,128]{2,1,0:T(8,128)S(1)} %bitcast.13), custom_call_target="tpu_custom_call" | custom-call | flops 1800000000 | bytes 5399999 | tf_op jit(solution)/shard_map/adjoint_state/pallas_call | solution.py:628
  35.4 2.5 %collective-permute-start.3 = (f32[4,16,128]{2,1,0:T(8,128)S(1)}, f32[4,16,128]{2,1,0:T(8,128)S(1)}, u32[]{:S(2)}, u32[]{:S(2)}) collective-permute-start(f32[4,16,128]{2,1,0:T(8,128)S(1)} %get-tuple-element.107), channel_id=1, source_target_pairs={{0,63},{1,2},{2,1},{3,4},{4,3},{5,6},{6,5},{7,8},{8,7},{9,10},{10,... | collective-permute-start | bytes 98312 | tf_op jit(solution)/shard_map/ppermute | solution.py:708
  37.9 3.9 %prepare2.1 = (bf16[16,128,256]{2,1,0:T(8,128)(2,1)S(1)}, f32[16,16,128]{2,1,0:T(8,128)S(1)}) custom-call(f32[4,3,16,4096]{3,2,1,0:T(8,128)} %bitcast.17, f32[4,16,4096]{2,1,0:T(8,128)} %dinv_hbm.3, f32[4,16,1024]{2,1,0:T(8,128)} %rhs_hbm.3), custom_call_target="tpu_custom_call" | custom-call | flops 2500000000 | bytes 7500000 | tf_op jit(solution)/shard_map/prepare2/pallas_call | solution.py:603
  42.9 2.5 %collective-permute-start.9 = (f32[4,16,128]{2,1,0:T(8,128)S(1)}, f32[4,16,128]{2,1,0:T(8,128)S(1)}, u32[]{:S(2)}, u32[]{:S(2)}) collective-permute-start(f32[4,16,128]{2,1,0:T(8,128)S(1)} %get-tuple-element.108), channel_id=1, source_target_pairs={{0,63},{1,2},{2,1},{3,4},{4,3},{5,6},{6,5},{7,8},{8,7},{9,10},{10,... | collective-permute-start | bytes 98312 | tf_op jit(solution)/shard_map/ppermute | solution.py:708
  45.4 3.9 %prepare3.1 = (bf16[16,128,256]{2,1,0:T(8,128)(2,1)S(1)}, f32[16,16,128]{2,1,0:T(8,128)S(1)}) custom-call(f32[4,3,16,4096]{3,2,1,0:T(8,128)} %bitcast.18, f32[4,16,4096]{2,1,0:T(8,128)} %dinv_hbm.3, f32[4,16,1024]{2,1,0:T(8,128)} %rhs_hbm.3), custom_call_target="tpu_custom_call" | custom-call | flops 2500000000 | bytes 7500000 | tf_op jit(solution)/shard_map/prepare3/pallas_call | solution.py:603
  52.8 2.1 %collective-permute-start.12 = (f32[4,16,128]{2,1,0:T(8,128)S(1)}, f32[4,16,128]{2,1,0:T(8,128)S(1)}, u32[]{:S(2)}, u32[]{:S(2)}) collective-permute-start(f32[4,16,128]{2,1,0:T(8,128)S(1)} %get-tuple-element.132), channel_id=1, source_target_pairs={{0,127},{1,64},{2,65},{3,66},{4,67},{5,68},{6,69},{7,70},{8,71},{9... | collective-permute-start | bytes 98312 | tf_op jit(solution)/shard_map/ppermute | solution.py:715
  58.5 4.7 %collective-permute-done.14.refs_6_ = f32[4,16,128]{2,1,0:T(8,128)S(1)} collective-permute-done((f32[4,16,128]{2,1,0:T(8,128)S(1)}, f32[4,16,128]{2,1,0:T(8,128)S(1)}, u32[]{:S(2)}, u32[]{:S(2)}) %collective-permute-start.14) | collective-permute-done | bytes 32800 | tf_op jit(solution)/shard_map/ppermute | solution.py:708
  65.1 4.7 %collective-permute-done.16.refs_6_ = f32[4,16,128]{2,1,0:T(8,128)S(1)} collective-permute-done((f32[4,16,128]{2,1,0:T(8,128)S(1)}, f32[4,16,128]{2,1,0:T(8,128)S(1)}, u32[]{:S(2)}, u32[]{:S(2)}) %collective-permute-start.16) | collective-permute-done | bytes 32800 | tf_op jit(solution)/shard_map/ppermute | solution.py:708
  71.8 3.6 %ghost_send.3 = (f32[8,112,128]{2,1,0:T(8,128)S(1)}, f32[8,112,128]{2,1,0:T(8,128)S(1)}) custom-call(s32[16,128]{1,0:T(8,128)S(4)} %get-tuple-element.88.s_ref.refs_0_, bf16[16,128,256]{2,1,0:T(8,128)(2,1)S(1)} %get-tuple-element.120.w_ref.refs_1_.w0_ref, f32[16,16,128]{2,1,0:T(8,128)S(1)} %get-tuple-element.121.r_ref.refs_2_.r0_ref, ...), custom_call_target="tpu_custom_call" | custom-call | flops 500000000 | bytes 1500000 | tf_op jit(solution)/shard_map/ghost_send/pallas_call | solution.py:628
  75.4 3.2 %collective-permute-start.7 = (f32[8,112,128]{2,1,0:T(8,128)S(1)}, f32[8,112,128]{2,1,0:T(8,128)S(1)}, u32[]{:S(2)}, u32[]{:S(2)}) collective-permute-start(f32[8,112,128]{2,1,0:T(8,128)S(1)} %get-tuple-element.124), channel_id=1, source_target_pairs={{0,63},{1,2},{2,1},{3,4},{4,3},{5,6},{6,5},{7,8},{8,7},{9,10},{10,... | collective-permute-start | bytes 1376264 | tf_op jit(solution)/shard_map/ppermute | solution.py:708
  79.6 5.1 %collective-permute-done.19 = f32[2,8,16,128]{3,2,1,0:T(8,128)S(1)} collective-permute-done((f32[2,8,16,128]{3,2,1,0:T(8,128)S(1)}, f32[2,8,16,128]{3,2,1,0:T(8,128)S(1)}, u32[]{:S(2)}, u32[]{:S(2)}) %collective-permute-start.19) | collective-permute-done | bytes 131104 | tf_op jit(solution)/shard_map/ppermute | solution.py:720
  86.1 3.6 %ghost_send.2 = (f32[8,112,128]{2,1,0:T(8,128)S(1)}, f32[8,112,128]{2,1,0:T(8,128)S(1)}) custom-call(s32[16,128]{1,0:T(8,128)S(4)} %get-tuple-element.88.s_ref.refs_0_, bf16[16,128,256]{2,1,0:T(8,128)(2,1)S(1)} %get-tuple-element.109.refs_1_.w_ref.w0_ref, f32[16,16,128]{2,1,0:T(8,128)S(1)} %get-tuple-element.110.refs_2_.r_ref.r0_ref, ...), custom_call_target="tpu_custom_call" | custom-call | flops 500000000 | bytes 1500000 | tf_op jit(solution)/shard_map/ghost_send/pallas_call | solution.py:628
  90.2 3.8 %collective-permute-start.5 = (f32[8,112,128]{2,1,0:T(8,128)S(1)}, f32[8,112,128]{2,1,0:T(8,128)S(1)}, u32[]{:S(2)}, u32[]{:S(2)}) collective-permute-start(f32[8,112,128]{2,1,0:T(8,128)S(1)} %get-tuple-element.113), channel_id=1, source_target_pairs={{0,63},{1,2},{2,1},{3,4},{4,3},{5,6},{6,5},{7,8},{8,7},{9,10},{10,... | collective-permute-start | bytes 1376264 | tf_op jit(solution)/shard_map/ppermute | solution.py:708
  97.4 6.7 %rows0_0.1 = (f32[4,16,1024]{2,1,0:T(8,128)S(1)}, f32[4,16,1024]{2,1,0:T(8,128)S(1)}) custom-call(f32[16,16,128]{2,1,0:T(8,128)S(1)} %get-tuple-element.160.refs_0_, f32[16,16,128]{2,1,0:T(8,128)S(1)} %get-tuple-element.161.refs_1_, f32[16,16,128]{2,1,0:T(8,128)S(1)} %get-tuple-element.162.refs_2_, f32[16,16,128]{2,1,0:T(8,128)S(1)} %get-tuple-element.163.refs_3_), custom_call_target="tpu_custom_call" | custom-call | flops 2400000000 | bytes 7200000 | tf_op jit(solution)/shard_map/rows0_0/pallas_call | solution.py:628
  106.3 4.7 %collective-permute-start.24 = (f32[2,8,16,128]{3,2,1,0:T(8,128)S(1)}, f32[2,8,16,128]{3,2,1,0:T(8,128)S(1)}, u32[]{:S(2)}, u32[]{:S(2)}) collective-permute-start(f32[2,8,16,128]{3,2,1,0:T(8,128)S(1)} %get-tuple-element.145), channel_id=1, source_target_pairs={{0,64},{1,65},{2,66},{3,67},{4,68},{5,69},{6,70},{7,71},{8,72},{9,... | collective-permute-start | bytes 393224 | tf_op jit(solution)/shard_map/ppermute | solution.py:720
  111.0 2.9 %collective-permute-done.24 = f32[2,8,16,128]{3,2,1,0:T(8,128)S(1)} collective-permute-done((f32[2,8,16,128]{3,2,1,0:T(8,128)S(1)}, f32[2,8,16,128]{3,2,1,0:T(8,128)S(1)}, u32[]{:S(2)}, u32[]{:S(2)}) %collective-permute-start.24) | collective-permute-done | bytes 131104 | tf_op jit(solution)/shard_map/ppermute | solution.py:720
  115.8 5.3 %collective-permute-done.26.far_ref = f32[8,16,128]{2,1,0:T(8,128)S(1)} collective-permute-done((f32[8,16,128]{2,1,0:T(8,128)S(1)}, f32[8,16,128]{2,1,0:T(8,128)S(1)}, u32[]{:S(2)}, u32[]{:S(2)}) %collective-permute-start.26) | collective-permute-done | bytes 65568 | tf_op jit(solution)/shard_map/ppermute | solution.py:708
  124.6 3.4 %rows3_0.1 = (f32[4,16,1024]{2,1,0:T(8,128)S(1)}, f32[4,16,1024]{2,1,0:T(8,128)S(1)}) custom-call(f32[16,16,128]{2,1,0:T(8,128)S(1)} %get-tuple-element.150.refs_0_, f32[16,16,128]{2,1,0:T(8,128)S(1)} %get-tuple-element.151.refs_1_, f32[4,16,1024]{2,1,0:T(8,128)S(1)} %get-tuple-element.170.refs_2_, ...), custom_call_target="tpu_custom_call", output_to_operand_aliasing={{0}: (2, {}), {1}: (3, {})} | custom-call | flops 1200000000 | bytes 3600000 | tf_op jit(solution)/shard_map/rows3_0/pallas_call | solution.py:628
  129.8 2.2 %pair3_2.1 = (f32[16,16,128]{2,1,0:T(8,128)S(1)}, f32[16,16,128]{2,1,0:T(8,128)S(1)}, f32[2,8,16,128]{3,2,1,0:T(8,128)}) custom-call(s32[16,128]{1,0:T(8,128)S(4)} %get-tuple-element.88.s_ref.refs_0_, s32[16,128]{1,0:T(8,128)S(4)} %get-tuple-element.114.ghost_s, bf16[16,128,256]{2,1,0:T(8,128)(2,1)S(1)} %get-tuple-element.109.refs_1_.w_ref.w0_ref, ...), custom_call_target="tpu_custom_call" | custom-call | flops 1800000000 | bytes 5400000 | tf_op jit(solution)/shard_map/pair3_2/pallas_call | solution.py:628
  131.9 3.7 %rows3_2.1 = (f32[4,16,1024]{2,1,0:T(8,128)S(1)}, f32[4,16,1024]{2,1,0:T(8,128)S(1)}) custom-call(f32[16,16,128]{2,1,0:T(8,128)S(1)} %get-tuple-element.148.refs_0_, f32[16,16,128]{2,1,0:T(8,128)S(1)} %get-tuple-element.149.refs_1_, f32[4,16,1024]{2,1,0:T(8,128)S(1)} %get-tuple-element.172.refs_2_, ...), custom_call_target="tpu_custom_call", output_to_operand_aliasing={{0}: (2, {}), {1}: (3, {})} | custom-call | flops 1200000000 | bytes 3600000 | tf_op jit(solution)/shard_map/rows3_2/pallas_call | solution.py:628
  (69 shorter events, 36.3 us)
Async XLA Ops:
  2.4 23.9 %all-to-all-start = ((f32[1,64,1024]{2,0,1:T(1,128)}), f32[1,64,1024]{2,0,1:T(1,128)S(1)}, u32[]{:S(2)}, u32[]{:S(2)}) async-start(f32[1,64,1024]{2,0,1:T(1,128)} %bitcast.14), calls=%async_computation | async-start | bytes 524288 | tf_op jit(solution)/shard_map/all_to_all | solution.py:698
  28.0 6.7 %collective-permute-start.1 = (f32[4,16,128]{2,1,0:T(8,128)S(1)}, f32[4,16,128]{2,1,0:T(8,128)S(1)}, u32[]{:S(2)}, u32[]{:S(2)}) collective-permute-start(f32[4,16,128]{2,1,0:T(8,128)S(1)} %get-tuple-element.97), channel_id=1, source_target_pairs={{0,63},{1,2},{2,1},{3,4},{4,3},{5,6},{6,5},{7,8},{8,7},{9,10},{10,... | collective-permute-start | bytes 98312 | tf_op jit(solution)/shard_map/ppermute | solution.py:708
  35.3 6.5 %collective-permute-start.2 = (f32[4,16,128]{2,1,0:T(8,128)S(1)}, f32[4,16,128]{2,1,0:T(8,128)S(1)}, u32[]{:S(2)}, u32[]{:S(2)}) collective-permute-start(f32[4,16,128]{2,1,0:T(8,128)S(1)} %get-tuple-element.106), channel_id=1, source_target_pairs={{0,1},{1,0},{2,3},{3,2},{4,5},{5,4},{6,7},{7,6},{8,9},{9,8},{10,11... | collective-permute-start | bytes 98312 | tf_op jit(solution)/shard_map/ppermute | solution.py:709
  35.4 6.7 %collective-permute-start.3 = (f32[4,16,128]{2,1,0:T(8,128)S(1)}, f32[4,16,128]{2,1,0:T(8,128)S(1)}, u32[]{:S(2)}, u32[]{:S(2)}) collective-permute-start(f32[4,16,128]{2,1,0:T(8,128)S(1)} %get-tuple-element.107), channel_id=1, source_target_pairs={{0,63},{1,2},{2,1},{3,4},{4,3},{5,6},{6,5},{7,8},{8,7},{9,10},{10,... | collective-permute-start | bytes 98312 | tf_op jit(solution)/shard_map/ppermute | solution.py:708
  42.8 6.5 %collective-permute-start.8 = (f32[4,16,128]{2,1,0:T(8,128)S(1)}, f32[4,16,128]{2,1,0:T(8,128)S(1)}, u32[]{:S(2)}, u32[]{:S(2)}) collective-permute-start(f32[4,16,128]{2,1,0:T(8,128)S(1)} %get-tuple-element.129), channel_id=1, source_target_pairs={{0,1},{1,0},{2,3},{3,2},{4,5},{5,4},{6,7},{7,6},{8,9},{9,8},{10,11... | collective-permute-start | bytes 98312 | tf_op jit(solution)/shard_map/ppermute | solution.py:709
  42.9 6.7 %collective-permute-start.9 = (f32[4,16,128]{2,1,0:T(8,128)S(1)}, f32[4,16,128]{2,1,0:T(8,128)S(1)}, u32[]{:S(2)}, u32[]{:S(2)}) collective-permute-start(f32[4,16,128]{2,1,0:T(8,128)S(1)} %get-tuple-element.108), channel_id=1, source_target_pairs={{0,63},{1,2},{2,1},{3,4},{4,3},{5,6},{6,5},{7,8},{8,7},{9,10},{10,... | collective-permute-start | bytes 98312 | tf_op jit(solution)/shard_map/ppermute | solution.py:708
  50.2 6.3 %collective-permute-start.10 = (f32[8,16,128]{2,1,0:T(8,128)S(1)}, f32[8,16,128]{2,1,0:T(8,128)S(1)}, u32[]{:S(2)}, u32[]{:S(2)}) collective-permute-start(f32[8,16,128]{2,1,0:T(8,128)S(1)} %get-tuple-element.130), channel_id=1, source_target_pairs={{0,64},{1,65},{2,66},{3,67},{4,68},{5,69},{6,70},{7,71},{8,72},{9,... | collective-permute-start | bytes 196616 | tf_op jit(solution)/shard_map/ppermute | solution.py:715
  56.5 6.7 %collective-permute-start.14 = (f32[4,16,128]{2,1,0:T(8,128)S(1)}, f32[4,16,128]{2,1,0:T(8,128)S(1)}, u32[]{:S(2)}, u32[]{:S(2)}) collective-permute-start(f32[4,16,128]{2,1,0:T(8,128)S(1)} %get-tuple-element.135), channel_id=1, source_target_pairs={{0,63},{1,2},{2,1},{3,4},{4,3},{5,6},{6,5},{7,8},{8,7},{9,10},{10,... | collective-permute-start | bytes 98312 | tf_op jit(solution)/shard_map/ppermute | solution.py:708
  63.2 6.7 %collective-permute-start.16 = (f32[4,16,128]{2,1,0:T(8,128)S(1)}, f32[4,16,128]{2,1,0:T(8,128)S(1)}, u32[]{:S(2)}, u32[]{:S(2)}) collective-permute-start(f32[4,16,128]{2,1,0:T(8,128)S(1)} %get-tuple-element.138), channel_id=1, source_target_pairs={{0,63},{1,2},{2,1},{3,4},{4,3},{5,6},{6,5},{7,8},{8,7},{9,10},{10,... | collective-permute-start | bytes 98312 | tf_op jit(solution)/shard_map/ppermute | solution.py:708
  69.8 8.7 %collective-permute-start.17 = (f32[4,16,128]{2,1,0:T(8,128)S(1)}, f32[4,16,128]{2,1,0:T(8,128)S(1)}, u32[]{:S(2)}, u32[]{:S(2)}) collective-permute-start(f32[4,16,128]{2,1,0:T(8,128)S(1)} %get-tuple-element.140), channel_id=1, source_target_pairs={{0,1},{1,0},{2,3},{3,2},{4,5},{5,4},{6,7},{7,6},{8,9},{9,8},{10,11... | collective-permute-start | bytes 98312 | tf_op jit(solution)/shard_map/ppermute | solution.py:709
  69.8 8.7 %collective-permute-start.18 = (f32[4,16,128]{2,1,0:T(8,128)S(1)}, f32[4,16,128]{2,1,0:T(8,128)S(1)}, u32[]{:S(2)}, u32[]{:S(2)}) collective-permute-start(f32[4,16,128]{2,1,0:T(8,128)S(1)} %get-tuple-element.141), channel_id=1, source_target_pairs={{0,63},{1,2},{2,1},{3,4},{4,3},{5,6},{6,5},{7,8},{8,7},{9,10},{10,... | collective-permute-start | bytes 98312 | tf_op jit(solution)/shard_map/ppermute | solution.py:708
  75.4 14.8 %collective-permute-start.6 = (f32[8,112,128]{2,1,0:T(8,128)S(1)}, f32[8,112,128]{2,1,0:T(8,128)S(1)}, u32[]{:S(2)}, u32[]{:S(2)}) collective-permute-start(f32[8,112,128]{2,1,0:T(8,128)S(1)} %get-tuple-element.123), channel_id=1, source_target_pairs={{0,1},{1,0},{2,3},{3,2},{4,5},{5,4},{6,7},{7,6},{8,9},{9,8},{10,11... | collective-permute-start | bytes 1376264 | tf_op jit(solution)/shard_map/ppermute | solution.py:709
  75.4 18.6 %collective-permute-start.7 = (f32[8,112,128]{2,1,0:T(8,128)S(1)}, f32[8,112,128]{2,1,0:T(8,128)S(1)}, u32[]{:S(2)}, u32[]{:S(2)}) collective-permute-start(f32[8,112,128]{2,1,0:T(8,128)S(1)} %get-tuple-element.124), channel_id=1, source_target_pairs={{0,63},{1,2},{2,1},{3,4},{4,3},{5,6},{6,5},{7,8},{8,7},{9,10},{10,... | collective-permute-start | bytes 1376264 | tf_op jit(solution)/shard_map/ppermute | solution.py:708
  78.6 6.2 %collective-permute-start.19 = (f32[2,8,16,128]{3,2,1,0:T(8,128)S(1)}, f32[2,8,16,128]{3,2,1,0:T(8,128)S(1)}, u32[]{:S(2)}, u32[]{:S(2)}) collective-permute-start(f32[2,8,16,128]{3,2,1,0:T(8,128)S(1)} %get-tuple-element.142), channel_id=1, source_target_pairs={{0,192},{1,193},{2,194},{3,195},{4,196},{5,197},{6,198},{7,199},{8... | collective-permute-start | bytes 393224 | tf_op jit(solution)/shard_map/ppermute | solution.py:720
  84.8 11.2 %collective-permute-start.21 = (f32[8,16,128]{2,1,0:T(8,128)S(1)}, f32[8,16,128]{2,1,0:T(8,128)S(1)}, u32[]{:S(2)}, u32[]{:S(2)}) collective-permute-start(f32[8,16,128]{2,1,0:T(8,128)S(1)} %get-tuple-element.176.own_far), channel_id=1, source_target_pairs={{0,63},{1,2},{2,1},{3,4},{4,3},{5,6},{6,5},{7,8},{8,7},{9,10},{10,... | collective-permute-start | bytes 196616 | tf_op jit(solution)/shard_map/ppermute | solution.py:708
  86.1 9.8 %collective-permute-start.20 = (f32[8,16,128]{2,1,0:T(8,128)S(1)}, f32[8,16,128]{2,1,0:T(8,128)S(1)}, u32[]{:S(2)}, u32[]{:S(2)}) collective-permute-start(f32[8,16,128]{2,1,0:T(8,128)S(1)} %get-tuple-element.177.own_near), channel_id=1, source_target_pairs={{0,1},{1,0},{2,3},{3,2},{4,5},{5,4},{6,7},{7,6},{8,9},{9,8},{10,11... | collective-permute-start | bytes 196616 | tf_op jit(solution)/shard_map/ppermute | solution.py:709
  89.7 14.4 %collective-permute-start.4 = (f32[8,112,128]{2,1,0:T(8,128)S(1)}, f32[8,112,128]{2,1,0:T(8,128)S(1)}, u32[]{:S(2)}, u32[]{:S(2)}) collective-permute-start(f32[8,112,128]{2,1,0:T(8,128)S(1)} %get-tuple-element.112), channel_id=1, source_target_pairs={{0,1},{1,0},{2,3},{3,2},{4,5},{5,4},{6,7},{7,6},{8,9},{9,8},{10,11... | collective-permute-start | bytes 1376264 | tf_op jit(solution)/shard_map/ppermute | solution.py:709
  90.2 13.9 %collective-permute-start.5 = (f32[8,112,128]{2,1,0:T(8,128)S(1)}, f32[8,112,128]{2,1,0:T(8,128)S(1)}, u32[]{:S(2)}, u32[]{:S(2)}) collective-permute-start(f32[8,112,128]{2,1,0:T(8,128)S(1)} %get-tuple-element.113), channel_id=1, source_target_pairs={{0,63},{1,2},{2,1},{3,4},{4,3},{5,6},{6,5},{7,8},{8,7},{9,10},{10,... | collective-permute-start | bytes 1376264 | tf_op jit(solution)/shard_map/ppermute | solution.py:708
  96.0 10.1 %collective-permute-start.22 = (f32[8,16,128]{2,1,0:T(8,128)S(1)}, f32[8,16,128]{2,1,0:T(8,128)S(1)}, u32[]{:S(2)}, u32[]{:S(2)}) collective-permute-start(f32[8,16,128]{2,1,0:T(8,128)S(1)} %get-tuple-element.143.own_near), channel_id=1, source_target_pairs={{0,1},{1,0},{2,3},{3,2},{4,5},{5,4},{6,7},{7,6},{8,9},{9,8},{10,11... | collective-permute-start | bytes 196616 | tf_op jit(solution)/shard_map/ppermute | solution.py:709
  96.1 10.0 %collective-permute-start.23 = (f32[8,16,128]{2,1,0:T(8,128)S(1)}, f32[8,16,128]{2,1,0:T(8,128)S(1)}, u32[]{:S(2)}, u32[]{:S(2)}) collective-permute-start(f32[8,16,128]{2,1,0:T(8,128)S(1)} %get-tuple-element.144.own_far), channel_id=1, source_target_pairs={{0,63},{1,2},{2,1},{3,4},{4,3},{5,6},{6,5},{7,8},{8,7},{9,10},{10,... | collective-permute-start | bytes 196616 | tf_op jit(solution)/shard_map/ppermute | solution.py:708
  106.3 7.6 %collective-permute-start.24 = (f32[2,8,16,128]{3,2,1,0:T(8,128)S(1)}, f32[2,8,16,128]{3,2,1,0:T(8,128)S(1)}, u32[]{:S(2)}, u32[]{:S(2)}) collective-permute-start(f32[2,8,16,128]{3,2,1,0:T(8,128)S(1)} %get-tuple-element.145), channel_id=1, source_target_pairs={{0,64},{1,65},{2,66},{3,67},{4,68},{5,69},{6,70},{7,71},{8,72},{9,... | collective-permute-start | bytes 393224 | tf_op jit(solution)/shard_map/ppermute | solution.py:720
  114.0 7.1 %collective-permute-start.26 = (f32[8,16,128]{2,1,0:T(8,128)S(1)}, f32[8,16,128]{2,1,0:T(8,128)S(1)}, u32[]{:S(2)}, u32[]{:S(2)}) collective-permute-start(f32[8,16,128]{2,1,0:T(8,128)S(1)} %get-tuple-element.174.own_far), channel_id=1, source_target_pairs={{0,63},{1,2},{2,1},{3,4},{4,3},{5,6},{6,5},{7,8},{8,7},{9,10},{10,... | collective-permute-start | bytes 196616 | tf_op jit(solution)/shard_map/ppermute | solution.py:708
  122.6 5.4 %collective-permute-start.27 = (f32[8,16,128]{2,1,0:T(8,128)S(1)}, f32[8,16,128]{2,1,0:T(8,128)S(1)}, u32[]{:S(2)}, u32[]{:S(2)}) collective-permute-start(f32[8,16,128]{2,1,0:T(8,128)S(1)} %get-tuple-element.146.own_near), channel_id=1, source_target_pairs={{0,1},{1,0},{2,3},{3,2},{4,5},{5,4},{6,7},{7,6},{8,9},{9,8},{10,11... | collective-permute-start | bytes 196616 | tf_op jit(solution)/shard_map/ppermute | solution.py:709
  122.7 7.1 %collective-permute-start.28 = (f32[8,16,128]{2,1,0:T(8,128)S(1)}, f32[8,16,128]{2,1,0:T(8,128)S(1)}, u32[]{:S(2)}, u32[]{:S(2)}) collective-permute-start(f32[8,16,128]{2,1,0:T(8,128)S(1)} %get-tuple-element.147.own_far), channel_id=1, source_target_pairs={{0,63},{1,2},{2,1},{3,4},{4,3},{5,6},{6,5},{7,8},{8,7},{9,10},{10,... | collective-permute-start | bytes 196616 | tf_op jit(solution)/shard_map/ppermute | solution.py:708
  (6 other events, 19.8 us)

commit v2 on v1

--- a/solution.py
+++ b/solution.py
@@ -499,7 +499,7 @@
 
 
 def rows_kernel(rnd, levels, *refs):
-    *refs, sol_ref, adj_ref, spread_ref = refs
+    *refs, sol_ref, adj_ref, spread_ref, lines = refs
     results = refs[:len(levels)]
     section = lax.axis_index("lvl")
     forward = section == rnd
@@ -515,20 +515,20 @@
             def one(chunk, carry):
                 part = spread_ref[chunk]
                 wide = jnp.where(mask, nt(hi, part) + nt(lo, part), 0.0)
-                value = jnp.sum(wide.reshape(RL, NV, 128), axis=1)
-                lanes = pl.ds(pl.multiple_of(chunk * 128, 128), 128)
+                lines[chunk] = jnp.sum(wide.reshape(RL, NV, 128), axis=1)
+                return carry
+
+            lax.fori_loop(0, B * NV // 128, one, 0, unroll=8 if rnd == LV - 1 and levels[0] else 2)
+            for chunk in range(B * NV // 128):
+                lanes = pl.ds(chunk * 128, 128)
 
                 @pl.when(forward)
                 def _():
-                    sol_ref[t, :, lanes] = value
+                    sol_ref[t, :, lanes] = lines[chunk]
 
                 @pl.when(jnp.logical_not(forward))
                 def _():
-                    adj_ref[LV - 1 - t, :, lanes] = value
-
-                return carry
-
-            lax.fori_loop(0, B * NV // 128, one, 0, unroll=4 if rnd == LV - 1 and levels[0] else 1)
+                    adj_ref[LV - 1 - t, :, lanes] = lines[chunk]
 
 
 def vspec():
@@ -680,7 +680,7 @@
     place = len(results)
     return call(partial(rows_kernel, rnd, levels), "rows%d_%d" % (rnd, levels[0]), 0.6 * len(levels),
                 [*results, *outs], [VMEM(OUT, F32)] * 2,
-                [VMEM((B * NV // 128, 128, 128), BF16)],
+                [VMEM((B * NV // 128, 128, 128), BF16), VMEM((B * NV // 128, RL, 128), F32)],
                 input_output_aliases={place: 0, place + 1: 1} if outs else {})
 
 

time: 137 us -> 135 us (0.985)
  Pallas kernels: 53.1 us -> 46.8 us
  starting transfers between devices: 49.1 us -> 51.4 us
    pallas_call x24, Pallas kernels: 35.6 us -> 29.3 us  [call(): pl.pallas_call(body, out_shape=tuple(shapes), in_specs=[spec(x) for x in...]
    ppermute x2, starting transfers between devices: 5.75 us -> 8.05 us  [handoff(): return lax.ppermute(msgs, ('lvl', 'cell'), pairs)]
  transfers between devices with their start and end apart: 30 -> 30, of which waited for: 11 -> 11; matrix products, arithmetic and copies ran while one was open for 0% -> 0% of each run, Pallas kernels for 29% -> 27%
where the time goes in v2:
time: 135 us; the launch traced here: 134 us
  starting transfers between devices  51.4 us (38%)
  Pallas kernels  46.8 us (35%)
  waiting for transfers between devices  33.7 us (25%)
  local copies, waits for them, and re-layouts  1.43 us (1%)
    pallas_call x24, Pallas kernels, call(): pl.pallas_call(body, out_shape=tuple(shapes), in_specs=[spec(x) for x in...  29.3 us
    ppermute x12, starting transfers between devices, exchange(): far_in = lax.ppermute(far, 'cell', list(enumerate(far_of)))  25.8 us
    ppermute x12, waiting for transfers between devices, exchange(): far_in = lax.ppermute(far, 'cell', list(enumerate(far_of)))  19.9 us
    pallas_call x4, Pallas kernels, prepare(): pl.pallas_call(partial(blocks_kernel, part), out_shape=shapes, in_specs=s...  15.7 us
    all_to_all x1, starting transfers between devices, per_device(): lax.all_to_all(sent.reshape(1, cells, B * NV), 'cell', split_axis=1, conc...  11.9 us
    ppermute x2, waiting for transfers between devices, handoff(): return lax.ppermute(msgs, ('lvl', 'cell'), pairs)  8.08 us
    ppermute x2, starting transfers between devices, handoff(): return lax.ppermute(msgs, ('lvl', 'cell'), pairs)  8.05 us
    ppermute x3, starting transfers between devices, shift_handoff(): return lax.ppermute(x, ('lvl', 'cell'), pairs)  4.67 us
  transfers between devices with their start and end apart: 30, of which 11 were waited for; matrix products, arithmetic and copies ran while one was open for 0% of the time, Pallas kernels for 27%

profile of v2, /device:TPU:24, one launch (start us, length us, event | category | flops | bytes accessed | tf_op | source)
XLA Modules:
  0.0 134.4 jit_solution(3376874199749317192)
XLA Ops:
  2.4 11.9 %all-to-all-start = ((f32[1,64,1024]{2,0,1:T(1,128)}), f32[1,64,1024]{2,0,1:T(1,128)S(1)}, u32[]{:S(2)}, u32[]{:S(2)}) async-start(f32[1,64,1024]{2,0,1:T(1,128)} %bitcast.14), calls=%async_computation | async-start | bytes 524288 | tf_op jit(solution)/shard_map/all_to_all | solution.py:698
  14.4 3.9 %prepare0.1 = (bf16[16,128,256]{2,1,0:T(8,128)(2,1)S(1)}, f32[16,16,128]{2,1,0:T(8,128)S(1)}) custom-call(f32[4,3,16,4096]{3,2,1,0:T(8,128)} %bitcast.15, f32[4,16,4096]{2,1,0:T(8,128)} %dinv_hbm.3, f32[4,16,1024]{2,1,0:T(8,128)} %rhs_hbm.3), custom_call_target="tpu_custom_call" | custom-call | flops 2500000000 | bytes 7500000 | tf_op jit(solution)/shard_map/prepare0/pallas_call | solution.py:603
  18.3 3.9 %prepare1.1 = (bf16[16,128,256]{2,1,0:T(8,128)(2,1)S(1)}, f32[16,16,128]{2,1,0:T(8,128)S(1)}) custom-call(f32[4,3,16,4096]{3,2,1,0:T(8,128)} %bitcast.16, f32[4,16,4096]{2,1,0:T(8,128)} %dinv_hbm.3, f32[4,16,1024]{2,1,0:T(8,128)} %rhs_hbm.3), custom_call_target="tpu_custom_call" | custom-call | flops 2500000000 | bytes 7500000 | tf_op jit(solution)/shard_map/prepare1/pallas_call | solution.py:603
  22.3 4.1 %all-to-all-done = f32[1,64,1024]{2,0,1:T(1,128)S(1)} async-done(((f32[1,64,1024]{2,0,1:T(1,128)}), f32[1,64,1024]{2,0,1:T(1,128)S(1)}, u32[]{:S(2)}, u32[]{:S(2)}) %all-to-all-start) | async-done | bytes 262176 | tf_op jit(solution)/shard_map/all_to_all | solution.py:698
  29.6 3.5 %adjoint_state.3 = (f32[16,16,128]{2,1,0:T(8,128)S(1)}, f32[16,16,128]{2,1,0:T(8,128)S(1)}, f32[16,16,128]{2,1,0:T(8,128)S(1)}) custom-call(s32[16,128]{1,0:T(8,128)S(4)} %get-tuple-element.88.s_ref.refs_0_, f32[64,8,128]{2,1,0:T(8,128)S(1)} %bitcast.13), custom_call_target="tpu_custom_call" | custom-call | flops 1800000000 | bytes 5399999 | tf_op jit(solution)/shard_map/adjoint_state/pallas_call | solution.py:628
  35.4 2.4 %collective-permute-start.3 = (f32[4,16,128]{2,1,0:T(8,128)S(1)}, f32[4,16,128]{2,1,0:T(8,128)S(1)}, u32[]{:S(2)}, u32[]{:S(2)}) collective-permute-start(f32[4,16,128]{2,1,0:T(8,128)S(1)} %get-tuple-element.107), channel_id=1, source_target_pairs={{0,63},{1,2},{2,1},{3,4},{4,3},{5,6},{6,5},{7,8},{8,7},{9,10},{10,... | collective-permute-start | bytes 98312 | tf_op jit(solution)/shard_map/ppermute | solution.py:708
  37.9 3.9 %prepare2.1 = (bf16[16,128,256]{2,1,0:T(8,128)(2,1)S(1)}, f32[16,16,128]{2,1,0:T(8,128)S(1)}) custom-call(f32[4,3,16,4096]{3,2,1,0:T(8,128)} %bitcast.17, f32[4,16,4096]{2,1,0:T(8,128)} %dinv_hbm.3, f32[4,16,1024]{2,1,0:T(8,128)} %rhs_hbm.3), custom_call_target="tpu_custom_call" | custom-call | flops 2500000000 | bytes 7500000 | tf_op jit(solution)/shard_map/prepare2/pallas_call | solution.py:603
  42.9 2.5 %collective-permute-start.9 = (f32[4,16,128]{2,1,0:T(8,128)S(1)}, f32[4,16,128]{2,1,0:T(8,128)S(1)}, u32[]{:S(2)}, u32[]{:S(2)}) collective-permute-start(f32[4,16,128]{2,1,0:T(8,128)S(1)} %get-tuple-element.108), channel_id=1, source_target_pairs={{0,63},{1,2},{2,1},{3,4},{4,3},{5,6},{6,5},{7,8},{8,7},{9,10},{10,... | collective-permute-start | bytes 98312 | tf_op jit(solution)/shard_map/ppermute | solution.py:708
  45.4 3.9 %prepare3.1 = (bf16[16,128,256]{2,1,0:T(8,128)(2,1)S(1)}, f32[16,16,128]{2,1,0:T(8,128)S(1)}) custom-call(f32[4,3,16,4096]{3,2,1,0:T(8,128)} %bitcast.18, f32[4,16,4096]{2,1,0:T(8,128)} %dinv_hbm.3, f32[4,16,1024]{2,1,0:T(8,128)} %rhs_hbm.3), custom_call_target="tpu_custom_call" | custom-call | flops 2500000000 | bytes 7500000 | tf_op jit(solution)/shard_map/prepare3/pallas_call | solution.py:603
  52.8 2.1 %collective-permute-start.12 = (f32[4,16,128]{2,1,0:T(8,128)S(1)}, f32[4,16,128]{2,1,0:T(8,128)S(1)}, u32[]{:S(2)}, u32[]{:S(2)}) collective-permute-start(f32[4,16,128]{2,1,0:T(8,128)S(1)} %get-tuple-element.132), channel_id=1, source_target_pairs={{0,127},{1,64},{2,65},{3,66},{4,67},{5,68},{6,69},{7,70},{8,71},{9... | collective-permute-start | bytes 98312 | tf_op jit(solution)/shard_map/ppermute | solution.py:715
  58.5 4.7 %collective-permute-done.14.refs_6_ = f32[4,16,128]{2,1,0:T(8,128)S(1)} collective-permute-done((f32[4,16,128]{2,1,0:T(8,128)S(1)}, f32[4,16,128]{2,1,0:T(8,128)S(1)}, u32[]{:S(2)}, u32[]{:S(2)}) %collective-permute-start.14) | collective-permute-done | bytes 32800 | tf_op jit(solution)/shard_map/ppermute | solution.py:708
  65.1 4.7 %collective-permute-done.16.refs_6_ = f32[4,16,128]{2,1,0:T(8,128)S(1)} collective-permute-done((f32[4,16,128]{2,1,0:T(8,128)S(1)}, f32[4,16,128]{2,1,0:T(8,128)S(1)}, u32[]{:S(2)}, u32[]{:S(2)}) %collective-permute-start.16) | collective-permute-done | bytes 32800 | tf_op jit(solution)/shard_map/ppermute | solution.py:708
  71.8 3.6 %ghost_send.3 = (f32[8,112,128]{2,1,0:T(8,128)S(1)}, f32[8,112,128]{2,1,0:T(8,128)S(1)}) custom-call(s32[16,128]{1,0:T(8,128)S(4)} %get-tuple-element.88.s_ref.refs_0_, bf16[16,128,256]{2,1,0:T(8,128)(2,1)S(1)} %get-tuple-element.120.w_ref.refs_1_.w0_ref, f32[16,16,128]{2,1,0:T(8,128)S(1)} %get-tuple-element.121.r_ref.refs_2_.r0_ref, ...), custom_call_target="tpu_custom_call" | custom-call | flops 500000000 | bytes 1500000 | tf_op jit(solution)/shard_map/ghost_send/pallas_call | solution.py:628
  75.4 3.2 %collective-permute-start.7 = (f32[8,112,128]{2,1,0:T(8,128)S(1)}, f32[8,112,128]{2,1,0:T(8,128)S(1)}, u32[]{:S(2)}, u32[]{:S(2)}) collective-permute-start(f32[8,112,128]{2,1,0:T(8,128)S(1)} %get-tuple-element.124), channel_id=1, source_target_pairs={{0,63},{1,2},{2,1},{3,4},{4,3},{5,6},{6,5},{7,8},{8,7},{9,10},{10,... | collective-permute-start | bytes 1376264 | tf_op jit(solution)/shard_map/ppermute | solution.py:708
  79.6 5.1 %collective-permute-done.19 = f32[2,8,16,128]{3,2,1,0:T(8,128)S(1)} collective-permute-done((f32[2,8,16,128]{3,2,1,0:T(8,128)S(1)}, f32[2,8,16,128]{3,2,1,0:T(8,128)S(1)}, u32[]{:S(2)}, u32[]{:S(2)}) %collective-permute-start.19) | collective-permute-done | bytes 131104 | tf_op jit(solution)/shard_map/ppermute | solution.py:720
  86.1 3.6 %ghost_send.2 = (f32[8,112,128]{2,1,0:T(8,128)S(1)}, f32[8,112,128]{2,1,0:T(8,128)S(1)}) custom-call(s32[16,128]{1,0:T(8,128)S(4)} %get-tuple-element.88.s_ref.refs_0_, bf16[16,128,256]{2,1,0:T(8,128)(2,1)S(1)} %get-tuple-element.109.refs_1_.w_ref.w0_ref, f32[16,16,128]{2,1,0:T(8,128)S(1)} %get-tuple-element.110.refs_2_.r_ref.r0_ref, ...), custom_call_target="tpu_custom_call" | custom-call | flops 500000000 | bytes 1500000 | tf_op jit(solution)/shard_map/ghost_send/pallas_call | solution.py:628
  90.2 3.8 %collective-permute-start.5 = (f32[8,112,128]{2,1,0:T(8,128)S(1)}, f32[8,112,128]{2,1,0:T(8,128)S(1)}, u32[]{:S(2)}, u32[]{:S(2)}) collective-permute-start(f32[8,112,128]{2,1,0:T(8,128)S(1)} %get-tuple-element.113), channel_id=1, source_target_pairs={{0,63},{1,2},{2,1},{3,4},{4,3},{5,6},{6,5},{7,8},{8,7},{9,10},{10,... | collective-permute-start | bytes 1376264 | tf_op jit(solution)/shard_map/ppermute | solution.py:708
  97.4 4.3 %rows0_0.1 = (f32[4,16,1024]{2,1,0:T(8,128)S(1)}, f32[4,16,1024]{2,1,0:T(8,128)S(1)}) custom-call(f32[16,16,128]{2,1,0:T(8,128)S(1)} %get-tuple-element.160.refs_0_, f32[16,16,128]{2,1,0:T(8,128)S(1)} %get-tuple-element.161.refs_1_, f32[16,16,128]{2,1,0:T(8,128)S(1)} %get-tuple-element.162.refs_2_, f32[16,16,128]{2,1,0:T(8,128)S(1)} %get-tuple-element.163.refs_3_), custom_call_target="tpu_custom_call" | custom-call | flops 2400000000 | bytes 7200000 | tf_op jit(solution)/shard_map/rows0_0/pallas_call | solution.py:628
  104.0 7.0 %collective-permute-start.24 = (f32[2,8,16,128]{3,2,1,0:T(8,128)S(1)}, f32[2,8,16,128]{3,2,1,0:T(8,128)S(1)}, u32[]{:S(2)}, u32[]{:S(2)}) collective-permute-start(f32[2,8,16,128]{3,2,1,0:T(8,128)S(1)} %get-tuple-element.145), channel_id=1, source_target_pairs={{0,64},{1,65},{2,66},{3,67},{4,68},{5,69},{6,70},{7,71},{8,72},{9,... | collective-permute-start | bytes 393224 | tf_op jit(solution)/shard_map/ppermute | solution.py:720
  111.0 2.9 %collective-permute-done.24 = f32[2,8,16,128]{3,2,1,0:T(8,128)S(1)} collective-permute-done((f32[2,8,16,128]{3,2,1,0:T(8,128)S(1)}, f32[2,8,16,128]{3,2,1,0:T(8,128)S(1)}, u32[]{:S(2)}, u32[]{:S(2)}) %collective-permute-start.24) | collective-permute-done | bytes 131104 | tf_op jit(solution)/shard_map/ppermute | solution.py:720
  115.8 5.3 %collective-permute-done.26.far_ref = f32[8,16,128]{2,1,0:T(8,128)S(1)} collective-permute-done((f32[8,16,128]{2,1,0:T(8,128)S(1)}, f32[8,16,128]{2,1,0:T(8,128)S(1)}, u32[]{:S(2)}, u32[]{:S(2)}) %collective-permute-start.26) | collective-permute-done | bytes 65568 | tf_op jit(solution)/shard_map/ppermute | solution.py:708
  124.6 2.2 %rows3_0.1 = (f32[4,16,1024]{2,1,0:T(8,128)S(1)}, f32[4,16,1024]{2,1,0:T(8,128)S(1)}) custom-call(f32[16,16,128]{2,1,0:T(8,128)S(1)} %get-tuple-element.150.refs_0_, f32[16,16,128]{2,1,0:T(8,128)S(1)} %get-tuple-element.151.refs_1_, f32[4,16,1024]{2,1,0:T(8,128)S(1)} %get-tuple-element.170.refs_2_, ...), custom_call_target="tpu_custom_call", output_to_operand_aliasing={{0}: (2, {}), {1}: (3, {})} | custom-call | flops 1200000000 | bytes 3600000 | tf_op jit(solution)/shard_map/rows3_0/pallas_call | solution.py:628
  126.8 3.0 %collective-permute-done.28.far_ref = f32[8,16,128]{2,1,0:T(8,128)S(1)} collective-permute-done((f32[8,16,128]{2,1,0:T(8,128)S(1)}, f32[8,16,128]{2,1,0:T(8,128)S(1)}, u32[]{:S(2)}, u32[]{:S(2)}) %collective-permute-start.28) | collective-permute-done | bytes 65568 | tf_op jit(solution)/shard_map/ppermute | solution.py:708
  129.8 2.2 %pair3_2.1 = (f32[16,16,128]{2,1,0:T(8,128)S(1)}, f32[16,16,128]{2,1,0:T(8,128)S(1)}, f32[2,8,16,128]{3,2,1,0:T(8,128)}) custom-call(s32[16,128]{1,0:T(8,128)S(4)} %get-tuple-element.88.s_ref.refs_0_, s32[16,128]{1,0:T(8,128)S(4)} %get-tuple-element.114.ghost_s, bf16[16,128,256]{2,1,0:T(8,128)(2,1)S(1)} %get-tuple-element.109.refs_1_.w_ref.w0_ref, ...), custom_call_target="tpu_custom_call" | custom-call | flops 1800000000 | bytes 5400000 | tf_op jit(solution)/shard_map/pair3_2/pallas_call | solution.py:628
  (69 shorter events, 35.6 us)
Async XLA Ops:
  2.4 23.9 %all-to-all-start = ((f32[1,64,1024]{2,0,1:T(1,128)}), f32[1,64,1024]{2,0,1:T(1,128)S(1)}, u32[]{:S(2)}, u32[]{:S(2)}) async-start(f32[1,64,1024]{2,0,1:T(1,128)} %bitcast.14), calls=%async_computation | async-start | bytes 524288 | tf_op jit(solution)/shard_map/all_to_all | solution.py:698
  28.0 6.7 %collective-permute-start.1 = (f32[4,16,128]{2,1,0:T(8,128)S(1)}, f32[4,16,128]{2,1,0:T(8,128)S(1)}, u32[]{:S(2)}, u32[]{:S(2)}) collective-permute-start(f32[4,16,128]{2,1,0:T(8,128)S(1)} %get-tuple-element.97), channel_id=1, source_target_pairs={{0,63},{1,2},{2,1},{3,4},{4,3},{5,6},{6,5},{7,8},{8,7},{9,10},{10,... | collective-permute-start | bytes 98312 | tf_op jit(solution)/shard_map/ppermute | solution.py:708
  35.3 6.5 %collective-permute-start.2 = (f32[4,16,128]{2,1,0:T(8,128)S(1)}, f32[4,16,128]{2,1,0:T(8,128)S(1)}, u32[]{:S(2)}, u32[]{:S(2)}) collective-permute-start(f32[4,16,128]{2,1,0:T(8,128)S(1)} %get-tuple-element.106), channel_id=1, source_target_pairs={{0,1},{1,0},{2,3},{3,2},{4,5},{5,4},{6,7},{7,6},{8,9},{9,8},{10,11... | collective-permute-start | bytes 98312 | tf_op jit(solution)/shard_map/ppermute | solution.py:709
  35.4 6.7 %collective-permute-start.3 = (f32[4,16,128]{2,1,0:T(8,128)S(1)}, f32[4,16,128]{2,1,0:T(8,128)S(1)}, u32[]{:S(2)}, u32[]{:S(2)}) collective-permute-start(f32[4,16,128]{2,1,0:T(8,128)S(1)} %get-tuple-element.107), channel_id=1, source_target_pairs={{0,63},{1,2},{2,1},{3,4},{4,3},{5,6},{6,5},{7,8},{8,7},{9,10},{10,... | collective-permute-start | bytes 98312 | tf_op jit(solution)/shard_map/ppermute | solution.py:708
  42.8 6.5 %collective-permute-start.8 = (f32[4,16,128]{2,1,0:T(8,128)S(1)}, f32[4,16,128]{2,1,0:T(8,128)S(1)}, u32[]{:S(2)}, u32[]{:S(2)}) collective-permute-start(f32[4,16,128]{2,1,0:T(8,128)S(1)} %get-tuple-element.129), channel_id=1, source_target_pairs={{0,1},{1,0},{2,3},{3,2},{4,5},{5,4},{6,7},{7,6},{8,9},{9,8},{10,11... | collective-permute-start | bytes 98312 | tf_op jit(solution)/shard_map/ppermute | solution.py:709
  42.9 6.7 %collective-permute-start.9 = (f32[4,16,128]{2,1,0:T(8,128)S(1)}, f32[4,16,128]{2,1,0:T(8,128)S(1)}, u32[]{:S(2)}, u32[]{:S(2)}) collective-permute-start(f32[4,16,128]{2,1,0:T(8,128)S(1)} %get-tuple-element.108), channel_id=1, source_target_pairs={{0,63},{1,2},{2,1},{3,4},{4,3},{5,6},{6,5},{7,8},{8,7},{9,10},{10,... | collective-permute-start | bytes 98312 | tf_op jit(solution)/shard_map/ppermute | solution.py:708
  50.2 6.3 %collective-permute-start.10 = (f32[8,16,128]{2,1,0:T(8,128)S(1)}, f32[8,16,128]{2,1,0:T(8,128)S(1)}, u32[]{:S(2)}, u32[]{:S(2)}) collective-permute-start(f32[8,16,128]{2,1,0:T(8,128)S(1)} %get-tuple-element.130), channel_id=1, source_target_pairs={{0,64},{1,65},{2,66},{3,67},{4,68},{5,69},{6,70},{7,71},{8,72},{9,... | collective-permute-start | bytes 196616 | tf_op jit(solution)/shard_map/ppermute | solution.py:715
  56.5 6.7 %collective-permute-start.14 = (f32[4,16,128]{2,1,0:T(8,128)S(1)}, f32[4,16,128]{2,1,0:T(8,128)S(1)}, u32[]{:S(2)}, u32[]{:S(2)}) collective-permute-start(f32[4,16,128]{2,1,0:T(8,128)S(1)} %get-tuple-element.135), channel_id=1, source_target_pairs={{0,63},{1,2},{2,1},{3,4},{4,3},{5,6},{6,5},{7,8},{8,7},{9,10},{10,... | collective-permute-start | bytes 98312 | tf_op jit(solution)/shard_map/ppermute | solution.py:708
  63.2 6.7 %collective-permute-start.16 = (f32[4,16,128]{2,1,0:T(8,128)S(1)}, f32[4,16,128]{2,1,0:T(8,128)S(1)}, u32[]{:S(2)}, u32[]{:S(2)}) collective-permute-start(f32[4,16,128]{2,1,0:T(8,128)S(1)} %get-tuple-element.138), channel_id=1, source_target_pairs={{0,63},{1,2},{2,1},{3,4},{4,3},{5,6},{6,5},{7,8},{8,7},{9,10},{10,... | collective-permute-start | bytes 98312 | tf_op jit(solution)/shard_map/ppermute | solution.py:708
  69.8 8.7 %collective-permute-start.17 = (f32[4,16,128]{2,1,0:T(8,128)S(1)}, f32[4,16,128]{2,1,0:T(8,128)S(1)}, u32[]{:S(2)}, u32[]{:S(2)}) collective-permute-start(f32[4,16,128]{2,1,0:T(8,128)S(1)} %get-tuple-element.140), channel_id=1, source_target_pairs={{0,1},{1,0},{2,3},{3,2},{4,5},{5,4},{6,7},{7,6},{8,9},{9,8},{10,11... | collective-permute-start | bytes 98312 | tf_op jit(solution)/shard_map/ppermute | solution.py:709
  69.8 8.7 %collective-permute-start.18 = (f32[4,16,128]{2,1,0:T(8,128)S(1)}, f32[4,16,128]{2,1,0:T(8,128)S(1)}, u32[]{:S(2)}, u32[]{:S(2)}) collective-permute-start(f32[4,16,128]{2,1,0:T(8,128)S(1)} %get-tuple-element.141), channel_id=1, source_target_pairs={{0,63},{1,2},{2,1},{3,4},{4,3},{5,6},{6,5},{7,8},{8,7},{9,10},{10,... | collective-permute-start | bytes 98312 | tf_op jit(solution)/shard_map/ppermute | solution.py:708
  75.4 14.8 %collective-permute-start.6 = (f32[8,112,128]{2,1,0:T(8,128)S(1)}, f32[8,112,128]{2,1,0:T(8,128)S(1)}, u32[]{:S(2)}, u32[]{:S(2)}) collective-permute-start(f32[8,112,128]{2,1,0:T(8,128)S(1)} %get-tuple-element.123), channel_id=1, source_target_pairs={{0,1},{1,0},{2,3},{3,2},{4,5},{5,4},{6,7},{7,6},{8,9},{9,8},{10,11... | collective-permute-start | bytes 1376264 | tf_op jit(solution)/shard_map/ppermute | solution.py:709
  75.4 18.6 %collective-permute-start.7 = (f32[8,112,128]{2,1,0:T(8,128)S(1)}, f32[8,112,128]{2,1,0:T(8,128)S(1)}, u32[]{:S(2)}, u32[]{:S(2)}) collective-permute-start(f32[8,112,128]{2,1,0:T(8,128)S(1)} %get-tuple-element.124), channel_id=1, source_target_pairs={{0,63},{1,2},{2,1},{3,4},{4,3},{5,6},{6,5},{7,8},{8,7},{9,10},{10,... | collective-permute-start | bytes 1376264 | tf_op jit(solution)/shard_map/ppermute | solution.py:708
  78.6 6.2 %collective-permute-start.19 = (f32[2,8,16,128]{3,2,1,0:T(8,128)S(1)}, f32[2,8,16,128]{3,2,1,0:T(8,128)S(1)}, u32[]{:S(2)}, u32[]{:S(2)}) collective-permute-start(f32[2,8,16,128]{3,2,1,0:T(8,128)S(1)} %get-tuple-element.142), channel_id=1, source_target_pairs={{0,192},{1,193},{2,194},{3,195},{4,196},{5,197},{6,198},{7,199},{8... | collective-permute-start | bytes 393224 | tf_op jit(solution)/shard_map/ppermute | solution.py:720
  84.8 11.2 %collective-permute-start.21 = (f32[8,16,128]{2,1,0:T(8,128)S(1)}, f32[8,16,128]{2,1,0:T(8,128)S(1)}, u32[]{:S(2)}, u32[]{:S(2)}) collective-permute-start(f32[8,16,128]{2,1,0:T(8,128)S(1)} %get-tuple-element.176.own_far), channel_id=1, source_target_pairs={{0,63},{1,2},{2,1},{3,4},{4,3},{5,6},{6,5},{7,8},{8,7},{9,10},{10,... | collective-permute-start | bytes 196616 | tf_op jit(solution)/shard_map/ppermute | solution.py:708
  86.1 9.8 %collective-permute-start.20 = (f32[8,16,128]{2,1,0:T(8,128)S(1)}, f32[8,16,128]{2,1,0:T(8,128)S(1)}, u32[]{:S(2)}, u32[]{:S(2)}) collective-permute-start(f32[8,16,128]{2,1,0:T(8,128)S(1)} %get-tuple-element.177.own_near), channel_id=1, source_target_pairs={{0,1},{1,0},{2,3},{3,2},{4,5},{5,4},{6,7},{7,6},{8,9},{9,8},{10,11... | collective-permute-start | bytes 196616 | tf_op jit(solution)/shard_map/ppermute | solution.py:709
  89.7 12.1 %collective-permute-start.4 = (f32[8,112,128]{2,1,0:T(8,128)S(1)}, f32[8,112,128]{2,1,0:T(8,128)S(1)}, u32[]{:S(2)}, u32[]{:S(2)}) collective-permute-start(f32[8,112,128]{2,1,0:T(8,128)S(1)} %get-tuple-element.112), channel_id=1, source_target_pairs={{0,1},{1,0},{2,3},{3,2},{4,5},{5,4},{6,7},{7,6},{8,9},{9,8},{10,11... | collective-permute-start | bytes 1376264 | tf_op jit(solution)/shard_map/ppermute | solution.py:709
  90.2 11.6 %collective-permute-start.5 = (f32[8,112,128]{2,1,0:T(8,128)S(1)}, f32[8,112,128]{2,1,0:T(8,128)S(1)}, u32[]{:S(2)}, u32[]{:S(2)}) collective-permute-start(f32[8,112,128]{2,1,0:T(8,128)S(1)} %get-tuple-element.113), channel_id=1, source_target_pairs={{0,63},{1,2},{2,1},{3,4},{4,3},{5,6},{6,5},{7,8},{8,7},{9,10},{10,... | collective-permute-start | bytes 1376264 | tf_op jit(solution)/shard_map/ppermute | solution.py:708
  96.0 7.8 %collective-permute-start.22 = (f32[8,16,128]{2,1,0:T(8,128)S(1)}, f32[8,16,128]{2,1,0:T(8,128)S(1)}, u32[]{:S(2)}, u32[]{:S(2)}) collective-permute-start(f32[8,16,128]{2,1,0:T(8,128)S(1)} %get-tuple-element.143.own_near), channel_id=1, source_target_pairs={{0,1},{1,0},{2,3},{3,2},{4,5},{5,4},{6,7},{7,6},{8,9},{9,8},{10,11... | collective-permute-start | bytes 196616 | tf_op jit(solution)/shard_map/ppermute | solution.py:709
  96.1 7.7 %collective-permute-start.23 = (f32[8,16,128]{2,1,0:T(8,128)S(1)}, f32[8,16,128]{2,1,0:T(8,128)S(1)}, u32[]{:S(2)}, u32[]{:S(2)}) collective-permute-start(f32[8,16,128]{2,1,0:T(8,128)S(1)} %get-tuple-element.144.own_far), channel_id=1, source_target_pairs={{0,63},{1,2},{2,1},{3,4},{4,3},{5,6},{6,5},{7,8},{8,7},{9,10},{10,... | collective-permute-start | bytes 196616 | tf_op jit(solution)/shard_map/ppermute | solution.py:708
  104.0 10.0 %collective-permute-start.24 = (f32[2,8,16,128]{3,2,1,0:T(8,128)S(1)}, f32[2,8,16,128]{3,2,1,0:T(8,128)S(1)}, u32[]{:S(2)}, u32[]{:S(2)}) collective-permute-start(f32[2,8,16,128]{3,2,1,0:T(8,128)S(1)} %get-tuple-element.145), channel_id=1, source_target_pairs={{0,64},{1,65},{2,66},{3,67},{4,68},{5,69},{6,70},{7,71},{8,72},{9,... | collective-permute-start | bytes 393224 | tf_op jit(solution)/shard_map/ppermute | solution.py:720
  114.0 7.1 %collective-permute-start.26 = (f32[8,16,128]{2,1,0:T(8,128)S(1)}, f32[8,16,128]{2,1,0:T(8,128)S(1)}, u32[]{:S(2)}, u32[]{:S(2)}) collective-permute-start(f32[8,16,128]{2,1,0:T(8,128)S(1)} %get-tuple-element.174.own_far), channel_id=1, source_target_pairs={{0,63},{1,2},{2,1},{3,4},{4,3},{5,6},{6,5},{7,8},{8,7},{9,10},{10,... | collective-permute-start | bytes 196616 | tf_op jit(solution)/shard_map/ppermute | solution.py:708
  115.8 5.3 %collective-permute-start.25 = (f32[8,16,128]{2,1,0:T(8,128)S(1)}, f32[8,16,128]{2,1,0:T(8,128)S(1)}, u32[]{:S(2)}, u32[]{:S(2)}) collective-permute-start(f32[8,16,128]{2,1,0:T(8,128)S(1)} %get-tuple-element.175.own_near), channel_id=1, source_target_pairs={{0,1},{1,0},{2,3},{3,2},{4,5},{5,4},{6,7},{7,6},{8,9},{9,8},{10,11... | collective-permute-start | bytes 196616 | tf_op jit(solution)/shard_map/ppermute | solution.py:709
  122.7 7.1 %collective-permute-start.28 = (f32[8,16,128]{2,1,0:T(8,128)S(1)}, f32[8,16,128]{2,1,0:T(8,128)S(1)}, u32[]{:S(2)}, u32[]{:S(2)}) collective-permute-start(f32[8,16,128]{2,1,0:T(8,128)S(1)} %get-tuple-element.147.own_far), channel_id=1, source_target_pairs={{0,63},{1,2},{2,1},{3,4},{4,3},{5,6},{6,5},{7,8},{8,7},{9,10},{10,... | collective-permute-start | bytes 196616 | tf_op jit(solution)/shard_map/ppermute | solution.py:708
  (6 other events, 18.8 us)
